TPU v7x, 32 devices: a whole 2x2x4 slice. The times are simulated.
32 devices in a mesh: slab: 8 (over z, y), chan: 4 (over x, core).
Axes of the slice: x: 2, y: 2, z: 4, core: 2. Of those that a mesh axis runs over, the one named last changes fastest.
Arguments:
- state_field: bfloat16 [2, 16, 256, 256, 256], P(None, 'chan', 'slab'), may hold values from -6 to 6
- spectral_weights: bfloat16 [16, 16, 64, 32, 2, 64], P(None, None, 'chan', None, None, 'slab'), may hold values from -1 to 1
- channel_shift: bfloat16 [16], P('chan'), may hold values from -3 to 3
Outputs:
- layer_output: bfloat16 [2, 16, 256, 256, 256], P(None, 'chan', 'slab')
All inputs are finite; a program needn't handle non-finite values.
Results may differ from a plain program's by a relative error of at most 0.015.
Values may be sent and summed in bfloat16 or wider, within the bound.
No kernel may reach another device: no remote copies, remote signals or barrier semaphores. Data moves between devices by JAX's collectives and lax.ppermute only.
A program may use at most 192 MiB of HBM per device.

v0:
```python
import jax
import jax.numpy as jnp
from jax import lax
from jax.sharding import PartitionSpec as P

NG = 256
KM = 32


def kept_freqs(mode_count, grid_side):
    index = jnp.arange(mode_count, dtype=jnp.int32)
    return jnp.where(index < mode_count // 2, index, index + grid_side - mode_count)


def angles(freq_list, grid_side):
    places = jnp.arange(grid_side, dtype=jnp.int32)
    product = freq_list[:, None] * places[None, :] % grid_side
    return product.astype(jnp.float32) * (2.0 * jnp.pi / grid_side)


def make_tables(grid_side, kept):
    bf = jnp.bfloat16
    fwd_scale = 1.0 / jnp.sqrt(jnp.float32(grid_side))
    inv_scale = 1.0 / jnp.sqrt(jnp.float32(2 * kept))
    z_freqs = jnp.arange(kept, dtype=jnp.int32)
    two_freqs = kept_freqs(2 * kept, grid_side)
    theta_z = angles(z_freqs, grid_side)
    theta_two = angles(two_freqs, grid_side)
    cos_z = jnp.cos(theta_z).T
    sin_z = jnp.sin(theta_z).T
    table_z = (jnp.stack([cos_z, -sin_z], -1) * fwd_scale).astype(bf)
    cos_t = jnp.cos(theta_two).T
    sin_t = jnp.sin(theta_two).T
    table_y = (
        jnp.stack([jnp.stack([cos_t, -sin_t], 1), jnp.stack([sin_t, cos_t], 1)], 0) * fwd_scale
    ).astype(bf)
    table_x = (
        jnp.stack([jnp.stack([cos_t, -sin_t], -1), jnp.stack([sin_t, cos_t], -1)], 1) * fwd_scale
    ).astype(bf)
    cos_m = jnp.cos(theta_two)
    sin_m = jnp.sin(theta_two)
    inv_x = (
        jnp.stack([jnp.stack([cos_m, sin_m], -1), jnp.stack([-sin_m, cos_m], -1)], 1) * inv_scale
    ).astype(bf)
    inv_y = (
        jnp.stack([jnp.stack([cos_m, sin_m], 1), jnp.stack([-sin_m, cos_m], 1)], 0) * inv_scale
    ).astype(bf)
    weight_k = jnp.where(z_freqs == 0, 1.0, 2.0).astype(jnp.float32)[:, None]
    inv_z = (
        jnp.stack([weight_k * jnp.cos(theta_z), -weight_k * jnp.sin(theta_z)], 1) * inv_scale
    ).astype(bf)
    return (table_z, table_y, table_x, inv_x, inv_y, inv_z)


def complex_mix(spec_part, wgt_part):
    f32 = jnp.float32
    spec_re = spec_part[..., 0, :]
    spec_im = spec_part[..., 1, :]
    wgt_re = wgt_part[..., 0, :]
    wgt_im = wgt_part[..., 1, :]
    mixed_re = jnp.einsum(
        "nimkj,iomkj->nomkj", spec_re, wgt_re, preferred_element_type=f32
    ) - jnp.einsum("nimkj,iomkj->nomkj", spec_im, wgt_im, preferred_element_type=f32)
    mixed_im = jnp.einsum(
        "nimkj,iomkj->nomkj", spec_re, wgt_im, preferred_element_type=f32
    ) + jnp.einsum("nimkj,iomkj->nomkj", spec_im, wgt_re, preferred_element_type=f32)
    return jnp.stack([mixed_re, mixed_im], -2)


def on_device(state_field, spectral_weights, channel_shift):
    f32 = jnp.float32
    bf = jnp.bfloat16
    table_z, table_y, table_x, inv_x, inv_y, inv_z = make_tables(NG, KM)
    coef_z = jnp.einsum(
        "bcxyz,zkp->bcxkpy", state_field, table_z, preferred_element_type=f32
    ).astype(bf)
    coef_y = jnp.einsum("bcxkpy,pyqn->bcxkqn", coef_z, table_y, preferred_element_type=f32).astype(
        bf
    )
    spectra = jnp.einsum(
        "bcxkpn,xpmq->bcmkqn",
        lax.all_to_all(coef_y, "slab", split_axis=5, concat_axis=2, tiled=True),
        table_x,
        preferred_element_type=f32,
    ).astype(bf)
    mixed = complex_mix(
        lax.all_to_all(spectra, "chan", split_axis=2, concat_axis=1, tiled=True), spectral_weights
    ).astype(bf)
    mixed_own = lax.all_to_all(mixed, "chan", split_axis=1, concat_axis=2, tiled=True)
    back_x = jnp.einsum("bcmkpn,mpxq->bcxkqn", mixed_own, inv_x, preferred_element_type=f32).astype(
        bf
    )
    back_y = jnp.einsum(
        "bcxkpn,pnqy->bcxkqy",
        lax.all_to_all(back_x, "slab", split_axis=2, concat_axis=5, tiled=True),
        inv_y,
        preferred_element_type=f32,
    ).astype(bf)
    summed = jnp.einsum("bcxkpy,kpz->bcxyz", back_y, inv_z, preferred_element_type=f32)
    shifted = summed + channel_shift.astype(f32)[None, :, None, None, None]
    return jax.nn.gelu(shifted, approximate=False).astype(bf)


def solution(mesh):
    return jax.shard_map(
        on_device,
        mesh=mesh,
        in_specs=(
            P(None, "chan", "slab", None, None),
            P(None, None, "chan", None, None, "slab"),
            P("chan"),
        ),
        out_specs=P(None, "chan", "slab", None, None),
        check_vma=False,
    )
```

profile of v0, /device:TPU:0, one launch (start us, length us, event | category | flops | bytes accessed | tf_op | source)
XLA Modules:
  0.0 565.5 jit_solution(4082622082239422644)
XLA Ops:
  0.0 0.1 sine_negate_fusion
  0.2 0.3 fusion.129
  0.5 18.6 %bitcast_convert_fusion.2 = bf16[2,4,32,32,2,64]{5,3,4,2,1,0:T(8,128)(2,1)} fusion(bf16[2,4,32,256,256]{4,3,2,1,0:T(8,128)(2,1)} %param.3, f32[1,256,2,64]{1,3,0,2:T(8,128)S(1)} %get-tuple-element.16, f32[1,256,2,64]{1,3,0,2:T(8,128)S(1)} %get-tuple-element.15, f32[256,32,1]{0,1,2:T(8,128)S(1)} %get-tuple-element.29, f32[256,32,1]{0,1,2:T(8,128)S(1)} %get-tuple-element.30), kind=kOutput, calls=%fused_computation.35 | convolution fusion | flops 3226714112 | bytes 35979264 | tf_op jit(solution)/shard_map/bcxkpy,pyqn->bcxkqn/dot_general | solution.py:77
  19.2 18.5 %copy.30 = bf16[2,4,32,32,2,64]{3,4,2,1,0,5:T(2,128)(2,1)} copy(bf16[2,4,32,32,2,64]{5,3,4,2,1,0:T(8,128)(2,1)} %bitcast_convert_fusion.2) | data formatting | bytes 4194304 | tf_op jit(solution)/shard_map/convert_element_type | solution.py:77
  37.7 11.2 %reshape.697 = bf16[8,2,65536]{2,1,0:T(2,128)(2,1)} reshape(bf16[64,2,4,32,2,32]{5,4,3,2,1,0:T(2,128)(2,1)} %bitcast.199) | data formatting | bytes 4194304
  48.9 7.5 %all-to-all-start = ((bf16[8,2,65536]{2,1,0:T(2,128)(2,1)}), bf16[8,2,65536]{2,1,0:T(2,128)(2,1)S(1)}, u32[]{:S(2)}, u32[]{:S(2)}) async-start(bf16[8,2,65536]{2,1,0:T(2,128)(2,1)} %reshape.697), calls=%async_computation | async-start | bytes 4194304 | tf_op jit(solution)/shard_map/all_to_all | solution.py:82
  56.4 0.3 fusion.128
  56.7 47.8 %all-to-all-done = bf16[8,2,65536]{2,1,0:T(2,128)(2,1)S(1)} async-done(((bf16[8,2,65536]{2,1,0:T(2,128)(2,1)}), bf16[8,2,65536]{2,1,0:T(2,128)(2,1)S(1)}, u32[]{:S(2)}, u32[]{:S(2)}) %all-to-all-start) | async-done | bytes 2097184 | tf_op jit(solution)/shard_map/all_to_all | solution.py:82
  104.5 6.4 %reshape.698 = bf16[64,2,4,32,2,32]{5,4,3,2,1,0:T(2,128)(2,1)} reshape(bf16[8,2,65536]{2,1,0:T(2,128)(2,1)S(1)} %all-to-all-done) | data formatting | bytes 4194304
  110.9 16.4 %copy.83 = bf16[2,4,32,32,2,64]{3,5,4,2,1,0:T(8,128)(2,1)} copy(bf16[2,4,32,32,2,64]{3,4,2,1,0,5:T(2,128)(2,1)} %bitcast.202) | data formatting | bytes 4194304 | tf_op jit(solution)/shard_map/all_to_all | solution.py:82
  127.4 17.4 %copy.32 = bf16[2,4,8,32,32,2,8]{3,2,4,5,6,1,0:T(8,128)(2,1)} copy(bf16[2,4,8,32,32,2,8]{4,6,2,5,3,1,0:T(8,128)(2,1)} %bitcast.203) | data formatting | bytes 4194304 | tf_op jit(solution)/shard_map/all_to_all | solution.py:82
  144.8 10.1 %reshape.686 = bf16[2,4,256,32,2,8,1]{2,3,4,5,1,0,6:T(8,128)(2,1)S(1)} reshape(bf16[2,4,8,32,32,2,8]{3,2,4,5,6,1,0:T(8,128)(2,1)} %copy.32) | data formatting | bytes 4194304 | tf_op jit(solution)/shard_map/all_to_all | solution.py:82
  154.9 0.7 fusion.53
  155.7 3.2 copy.33
  158.9 2.9 reshape.699
  161.9 3.5 all-to-all-start.1
  165.3 12.0 %fusion.145 = (bf16[16,16,16,32,1,8]{3,5,4,2,1,0:T(8,128)(2,1)}, bf16[16,16,16,32,1,8]{3,5,4,2,1,0:T(8,128)(2,1)}) fusion(bf16[16,16,16,32,2,8]{3,5,4,2,1,0:T(8,128)(2,1)} %param.4), kind=kLoop, calls=%fused_computation.166 | loop fusion | bytes 8388608 | tf_op jit(solution)/shard_map/slice | solution.py:59
  177.3 28.7 %copy.67 = bf16[16,16,16,32,1,8]{1,0,5,3,2,4:T(8,128)(2,1)} copy(bf16[16,16,16,32,1,8]{3,5,4,2,1,0:T(8,128)(2,1)} %get-tuple-element.5) | data formatting | bytes 4194304
  206.1 28.7 %copy.69 = bf16[16,16,16,32,1,8]{1,0,5,3,2,4:T(8,128)(2,1)} copy(bf16[16,16,16,32,1,8]{3,5,4,2,1,0:T(8,128)(2,1)} %get-tuple-element.6) | data formatting | bytes 4194304
  234.8 0.0 all-to-all-done.1
  234.8 1.1 reshape.700
  235.9 0.6 copy.35
  236.5 0.6 fusion.146
  237.1 4.3 copy.68
  241.4 2.3 copy.66
  243.8 0.0 copy-start
  243.8 9.5 %fusion.12 = f32[16,32,8,2,16]{4,3,2,1,0:T(2,128)} fusion(bf16[16,16,16,32,1,8]{1,0,5,3,2,4:T(8,128)(2,1)} %copy.69, bf16[2,16,16,32,1,8]{1,0,5,3,2,4:T(2,128)(2,1)S(1)} %copy.66), kind=kOutput, calls=%fused_computation.23 | convolution fusion | flops 4194304 | bytes 2883584 | tf_op jit(solution)/shard_map/nimkj,iomkj->nomkj/dot_general | solution.py:64
  253.3 8.7 %fusion.14 = f32[16,32,8,2,16]{4,3,2,1,0:T(2,128)S(1)} fusion(bf16[16,16,16,32,1,8]{1,0,5,3,2,4:T(8,128)(2,1)} %copy.69, bf16[2,16,16,32,1,8]{1,0,5,3,2,4:T(2,128)(2,1)} %copy.68), kind=kOutput, calls=%fused_computation.25 | convolution fusion | flops 4194304 | bytes 2883584 | tf_op jit(solution)/shard_map/nimkj,iomkj->nomkj/dot_general | solution.py:63
  262.0 0.0 copy-done
  262.1 9.3 %fusion.41 = bf16[2,16,16,32,1,8]{1,0,5,3,2,4:T(2,128)(2,1)S(1)} fusion(f32[16,32,8,2,16]{4,3,2,1,0:T(2,128)} %fusion.12, bf16[16,16,16,32,1,8]{1,0,5,3,2,4:T(8,128)(2,1)} %copy.67, bf16[2,16,16,32,1,8]{1,0,5,3,2,4:T(2,128)(2,1)S(1)} %copy-done), kind=kOutput, calls=%fused_computation.44 | convolution fusion | flops 4456448 | bytes 3145728 | tf_op jit(solution)/shard_map/nimkj,iomkj->nomkj/dot_general | solution.py:66
  271.4 8.3 %fusion.38 = bf16[2,16,16,32,1,8]{1,0,5,3,2,4:T(2,128)(2,1)S(1)} fusion(f32[16,32,8,2,16]{4,3,2,1,0:T(2,128)S(1)} %fusion.14, bf16[16,16,16,32,1,8]{1,0,5,3,2,4:T(8,128)(2,1)} %copy.67, bf16[2,16,16,32,1,8]{1,0,5,3,2,4:T(2,128)(2,1)S(1)} %copy.66), kind=kOutput, calls=%fused_computation.43 | convolution fusion | flops 4456448 | bytes 3145728 | tf_op jit(solution)/shard_map/nimkj,iomkj->nomkj/dot_general | solution.py:61
  279.7 0.0 copy-start.1
  279.7 9.0 %pad_maximum_fusion = bf16[2,16,16,32,2,8]{1,0,5,3,2,4:T(2,128)(2,1)} fusion(bf16[2,16,16,32,1,8]{1,0,5,3,2,4:T(2,128)(2,1)S(1)} %fusion.41, bf16[2,16,16,32,1,8]{1,0,5,3,2,4:T(2,128)(2,1)S(1)} %fusion.38), kind=kLoop, calls=%fused_computation.39 | loop fusion | flops 262144 | bytes 1048576 | tf_op jit(solution)/shard_map/stack | solution.py:67
  288.7 11.0 %copy.40 = bf16[2,16,16,32,2,8]{3,5,4,2,0,1:T(8,128)(2,1)S(1)} copy(bf16[2,16,16,32,2,8]{1,0,5,3,2,4:T(2,128)(2,1)} %pad_maximum_fusion) | data formatting | bytes 1048576 | tf_op jit(solution)/shard_map/stack | solution.py:67
  299.7 2.9 reshape.701
  302.6 3.7 all-to-all-start.2
  306.3 0.3 fusion.123
  306.7 8.4 %all-to-all-done.2 = bf16[4,2,32768]{2,1,0:T(2,128)(2,1)S(1)} async-done(((bf16[4,2,32768]{2,1,0:T(2,128)(2,1)}), bf16[4,2,32768]{2,1,0:T(2,128)(2,1)S(1)}, u32[]{:S(2)}, u32[]{:S(2)}) %all-to-all-start.2) | async-done | bytes 524320 | tf_op jit(solution)/shard_map/all_to_all | solution.py:89
  315.1 1.1 reshape.702
  316.2 1.7 copy.42
  317.9 2.8 copy.43
  320.7 0.8 fusion.52
  321.4 11.9 %copy.44 = bf16[2,4,256,32,2,8]{3,5,1,0,4,2:T(8,128)(2,1)} copy(bf16[2,4,256,32,2,8]{2,3,5,1,0,4:T(8,128)(2,1)S(1)} %fusion.52) | data formatting | bytes 4194304 | tf_op jit(solution)/shard_map/convert_element_type | solution.py:90
  333.4 11.2 %reshape.703 = bf16[8,2,65536]{2,1,0:T(2,128)(2,1)} reshape(bf16[256,2,2,4,8,32]{5,4,3,2,1,0:T(8,128)(2,1)} %bitcast.200) | data formatting | bytes 4194304
  344.5 3.6 all-to-all-start.3
  348.2 0.0 copy-done.1
  348.2 0.3 fusion.113
  348.6 0.1 sine_multiply_fusion
  348.8 47.6 %all-to-all-done.3 = bf16[8,2,65536]{2,1,0:T(2,128)(2,1)S(1)} async-done(((bf16[8,2,65536]{2,1,0:T(2,128)(2,1)}), bf16[8,2,65536]{2,1,0:T(2,128)(2,1)S(1)}, u32[]{:S(2)}, u32[]{:S(2)}) %all-to-all-start.3) | async-done | bytes 2097184 | tf_op jit(solution)/shard_map/all_to_all | solution.py:95
  396.4 6.4 %reshape.704 = bf16[256,2,2,4,8,32]{5,4,3,2,1,0:T(8,128)(2,1)} reshape(bf16[8,2,65536]{2,1,0:T(2,128)(2,1)S(1)} %all-to-all-done.3) | data formatting | bytes 4194304
  402.8 8.1 %bitcast_convert_fusion.8 = bf16[2,4,32,32,2,256]{5,3,4,2,1,0:T(8,128)(2,1)S(1)} fusion(bf16[2,4,8,32,32,2,8]{4,6,1,0,5,3,2:T(8,128)(2,1)} %bitcast.201, f32[1,64,2,256]{3,1,0,2:T(8,128)S(1)} %get-tuple-element.10, f32[1,64,2,256]{3,1,0,2:T(8,128)S(1)} %get-tuple-element.9), kind=kOutput, calls=%fused_computation.22.clone.clone.2 | convolution fusion | flops 1078132736 | bytes 10747904 | tf_op jit(solution)/shard_map/bcxkpn,pnqy->bcxkqy/dot_general | solution.py:93
  410.9 154.4 %fusion.2 = bf16[2,4,32,256,256]{4,3,2,1,0:T(8,128)(2,1)} fusion(f32[4]{0:T(128)S(1)} %convert_element_type.197, f32[32,1,256]{2,0,1:T(8,128)S(1)} %get-tuple-element.31, f32[32,1,256]{2,0,1:T(8,128)S(1)} %get-tuple-element.32, bf16[2,4,32,32,2,256]{5,3,4,2,1,0:T(8,128)(2,1)S(1)} %bitcast_convert_fusion.8), kind=kOutput, calls=%fused_computation.3 | convolution fusion | flops 3254829056 | bytes 42008592 | tf_op jit(solution)/shard_map/bcxkpy,kpz->bcxyz/dot_general | solution.py:99
  (8 shorter events, 0.1 us)
Async XLA Ops:
  48.9 55.7 %all-to-all-start = ((bf16[8,2,65536]{2,1,0:T(2,128)(2,1)}), bf16[8,2,65536]{2,1,0:T(2,128)(2,1)S(1)}, u32[]{:S(2)}, u32[]{:S(2)}) async-start(bf16[8,2,65536]{2,1,0:T(2,128)(2,1)} %reshape.697), calls=%async_computation | async-start | bytes 4194304 | tf_op jit(solution)/shard_map/all_to_all | solution.py:82
  161.9 73.0 %all-to-all-start.1 = ((bf16[4,2,32768]{2,1,0:T(2,128)(2,1)}), bf16[4,2,32768]{2,1,0:T(2,128)(2,1)S(1)}, u32[]{:S(2)}, u32[]{:S(2)}) async-start(bf16[4,2,32768]{2,1,0:T(2,128)(2,1)} %reshape.699), calls=%async_computation.1 | async-start | bytes 1048576 | tf_op jit(solution)/shard_map/all_to_all | solution.py:87
  243.8 18.3 %copy-start = (bf16[2,16,16,32,1,8]{1,0,5,3,2,4:T(2,128)(2,1)S(1)}, bf16[2,16,16,32,1,8]{1,0,5,3,2,4:T(2,128)(2,1)}, u32[]{:S(2)}) copy-start(bf16[2,16,16,32,1,8]{1,0,5,3,2,4:T(2,128)(2,1)} %copy.68) | copy-start | bytes 786436
  279.7 68.5 %copy-start.1 = (bf16[4]{0:T(256)(128)(2,1)S(1)}, bf16[4]{0:T(256)(128)(2,1)}, u32[]{:S(2)}) copy-start(bf16[4]{0:T(256)(128)(2,1)} %param.5) | copy-start | bytes 28
  302.6 12.5 %all-to-all-start.2 = ((bf16[4,2,32768]{2,1,0:T(2,128)(2,1)}), bf16[4,2,32768]{2,1,0:T(2,128)(2,1)S(1)}, u32[]{:S(2)}, u32[]{:S(2)}) async-start(bf16[4,2,32768]{2,1,0:T(2,128)(2,1)} %reshape.701), calls=%async_computation.2 | async-start | bytes 1048576 | tf_op jit(solution)/shard_map/all_to_all | solution.py:89
  344.5 51.8 %all-to-all-start.3 = ((bf16[8,2,65536]{2,1,0:T(2,128)(2,1)}), bf16[8,2,65536]{2,1,0:T(2,128)(2,1)S(1)}, u32[]{:S(2)}, u32[]{:S(2)}) async-start(bf16[8,2,65536]{2,1,0:T(2,128)(2,1)} %reshape.703), calls=%async_computation.3 | async-start | bytes 4194304 | tf_op jit(solution)/shard_map/all_to_all | solution.py:95
where the time goes:
time: 572 us; the launch traced here: 566 us
  matrix products  219 us (38%)
  local copies, waits for them, and re-layouts  214 us (37%)
  waiting for transfers between devices  104 us (18%)
  starting transfers between devices  18.3 us (3%)
  other arithmetic  10.8 us (2%)
    dot_general x1, matrix products, on_device(): jnp.einsum('bcxkpy,kpz->bcxyz', back_y, inv_z, preferred_element_type=f32)  154 us
    unnamed x16, local copies, waits for them, and re-layouts  107 us
    all_to_all x1, waiting for transfers between devices, on_device(): lax.all_to_all(coef_y, 'slab', split_axis=5, concat_axis=2, tiled=True)  47.8 us
    all_to_all x1, waiting for transfers between devices, on_device(): lax.all_to_all(back_x, 'slab', split_axis=2, concat_axis=5, tiled=True)  47.6 us
    all_to_all x3, local copies, waits for them, and re-layouts, on_device(): lax.all_to_all(coef_y, 'slab', split_axis=5, concat_axis=2, tiled=True)  44 us
    dot_general x1, matrix products, on_device(): jnp.einsum('bcxkpy,pyqn->bcxkqn', coef_z, table_y, preferred_element_type...  18.6 us
    convert_element_type x1, local copies, waits for them, and re-layouts, on_device(): jnp.einsum('bcxkpy,pyqn->bcxkqn', coef_z, table_y, preferred_element_type...  18.5 us
    slice x1, local copies, waits for them, and re-layouts, complex_mix(): wgt_re = wgt_part[..., 0, :]  12 us
  transfers between devices with their start and end apart: 4, of which 3 were waited for; matrix products, arithmetic and copies ran while one was open for 13% of the time, Pallas kernels for 0%

commit v1 on v0

v1 whole, which is shorter than its diff:
```python
import functools

import jax
import jax.numpy as jnp
import numpy as np
from jax import lax
from jax.experimental import pallas as pl
from jax.experimental.pallas import tpu as pltpu
from jax.sharding import PartitionSpec as P

NG = 256
KM = 32
F32 = jnp.float32
BF16 = jnp.bfloat16
VMEM_LIMIT = 48 * 1024 * 1024


def kept_freqs(mode_count, grid_side):
    index = np.arange(mode_count)
    return np.where(index < mode_count // 2, index, index + grid_side - mode_count)


def angles(freq_list, grid_side):
    product = freq_list[:, None] * np.arange(grid_side)[None, :] % grid_side
    return product.astype(np.float32) * np.float32(2.0 * np.pi / grid_side)


def make_tables(chans):
    two = 2 * KM
    fwd = np.float32(1.0) / np.sqrt(np.float32(NG))
    inv = np.float32(1.0) / np.sqrt(np.float32(two))
    theta_z = angles(np.arange(KM), NG)
    theta_two = angles(kept_freqs(two, NG), NG)
    cos_z, sin_z = np.cos(theta_z), np.sin(theta_z)
    cos_t, sin_t = np.cos(theta_two), np.sin(theta_two)
    lanes = 2 * chans * KM
    fwd_z = np.zeros((chans, NG, 2, chans, KM), np.float32)
    inv_z = np.zeros((chans, 2, chans, KM, NG), np.float32)
    weight_k = np.where(np.arange(KM) == 0, 1.0, 2.0).astype(np.float32)[:, None]
    for c in range(chans):
        fwd_z[c, :, 0, c, :] = cos_z.T * fwd
        fwd_z[c, :, 1, c, :] = -sin_z.T * fwd
        inv_z[c, 0, c] = weight_k * cos_z * inv
        inv_z[c, 1, c] = -weight_k * sin_z * inv
    fwd_z = fwd_z.reshape(chans * NG, lanes)
    inv_z = inv_z.reshape(chans, lanes, NG)
    fwd_two = np.concatenate([cos_t, sin_t], 0) * fwd
    inv_two = np.concatenate([cos_t.T, sin_t.T], 1) * inv
    return tuple(jnp.asarray(t, BF16) for t in (fwd_z, fwd_two, inv_two, inv_z))


def dot(a, b):
    return jnp.dot(a, b, preferred_element_type=F32)


def turn(rows):
    half = rows.shape[-1] // 2
    return jnp.concatenate([-rows[:, half:], rows[:, :half]], axis=1)


def unturn(twice):
    two, half = twice.shape[0] // 2, twice.shape[1] // 2
    cos_part, sin_part = twice[:two], twice[two:]
    return jnp.concatenate(
        [cos_part[:, :half] + sin_part[:, half:], cos_part[:, half:] - sin_part[:, :half]], axis=1
    )


def call(kernel, cost, **kwargs):
    flops, moved = cost
    return pl.pallas_call(
        kernel,
        compiler_params=pltpu.CompilerParams(vmem_limit_bytes=VMEM_LIMIT),
        cost_estimate=pl.CostEstimate(flops=flops, bytes_accessed=moved, transcendentals=0),
        **kwargs,
    )


def forward_zy(state, sample, slabs, fwd_z, fwd_two):
    _, chans, planes, _, _ = state.shape
    two = fwd_two.shape[0] // 2
    own = two // slabs
    lanes = fwd_z.shape[1]
    step = max(4, 16 // own)

    def kernel(state_ref, fwd_z_ref, fwd_two_ref, out_ref):
        found = []
        for x in range(step):
            plane = jnp.concatenate([state_ref[0, c, x] for c in range(chans)], axis=1)
            coef_z = dot(plane, fwd_z_ref[...]).astype(BF16)
            found.append(unturn(dot(fwd_two_ref[...], coef_z)).reshape(slabs, own, lanes))
        rows = jnp.stack(found, axis=1).reshape(slabs, step * own, lanes)
        out_ref[...] = rows.astype(BF16)

    return call(
        kernel,
        (2 * planes * NG * lanes * (chans * NG + 2 * two), 2 * chans * planes * NG * NG),
        grid=(planes // step,),
        in_specs=[
            pl.BlockSpec((1, chans, step, NG, NG), lambda i: (sample, 0, i, 0, 0)),
            pl.BlockSpec(fwd_z.shape, lambda i: (0, 0)),
            pl.BlockSpec(fwd_two.shape, lambda i: (0, 0)),
        ],
        out_specs=pl.BlockSpec((slabs, step * own, lanes), lambda i: (0, i, 0)),
        out_shape=jax.ShapeDtypeStruct((slabs, planes * own, lanes), BF16),
        name="forward_zy",
    )(state, fwd_z, fwd_two)


def forward_x(coef_y, groups, fwd_two):
    slabs, rows, lanes = coef_y.shape
    two = fwd_two.shape[0] // 2
    own = two // slabs
    half = lanes // 2
    part = two // groups

    def kernel(coef_ref, table_ref, out_ref, wide, found):
        flat = coef_ref[...].reshape(slabs * rows, lanes).astype(F32)
        wide[0] = flat[:, :half]
        wide[1] = flat[:, half:]
        for n in range(own):
            pick = pl.ds(n, NG, stride=own)
            planes = jnp.concatenate([wide[0, pick, :], wide[1, pick, :]], axis=1)
            modes = unturn(dot(table_ref[...], planes.astype(BF16)))
            put = pl.ds(n, two, stride=own)
            found[0, put, :] = modes[:, :half]
            found[1, put, :] = modes[:, half:]
        both = jnp.concatenate([found[0], found[1]], axis=1)
        out_ref[...] = both.reshape(groups, part * own, lanes).astype(BF16)

    return call(
        kernel,
        (4 * own * two * NG * lanes, 4 * slabs * rows * lanes),
        in_specs=[pl.BlockSpec(memory_space=pltpu.VMEM)] * 2,
        out_specs=pl.BlockSpec(memory_space=pltpu.VMEM),
        out_shape=jax.ShapeDtypeStruct((groups, part * own, lanes), BF16),
        scratch_shapes=[
            pltpu.VMEM((2, slabs * rows, half), F32),
            pltpu.VMEM((2, two * own, half), F32),
        ],
        name="forward_x",
    )(coef_y, fwd_two)


def place_weights(weights, chans):
    inputs, outputs, modes, _, own, kept = weights.shape
    groups = inputs // chans
    rows = modes * own
    lanes = chans * kept

    def kernel(w_ref, out_ref):
        for q in range(2):
            tiles = {}
            for i in range(chans):
                for o in range(chans):
                    tiles[i, o] = w_ref[i, o, :, q].astype(F32).reshape(rows, kept)
            for r in range(chans):
                row = jnp.concatenate([tiles[(o + r) % chans, o] for o in range(chans)], axis=1)
                out_ref[q, 0, 0, r] = row.astype(BF16)

    return call(
        kernel,
        (2 * weights.size, 10 * weights.size),
        grid=(groups, outputs // chans),
        in_specs=[
            pl.BlockSpec((chans, chans, modes, 2, own, kept), lambda i, o: (i, o, 0, 0, 0, 0))
        ],
        out_specs=pl.BlockSpec((2, 1, 1, chans, rows, lanes), lambda i, o: (0, i, o, 0, 0, 0)),
        out_shape=jax.ShapeDtypeStruct(
            (2, groups, outputs // chans, chans, rows, lanes), BF16
        ),
        name="place_weights",
    )(weights)


def mix(spectra, placed, kept):
    groups, rows, lanes = spectra.shape
    half = lanes // 2
    chans = placed.shape[3]
    step = 16

    def kernel(spec_ref, w_ref, out_ref):
        total = [[jnp.zeros((step, half), F32) for _ in range(2)] for _ in range(groups)]
        for i in range(groups):
            both = spec_ref[i].astype(F32)
            for r in range(chans):
                if r == 0:
                    re, im = both[:, :half], both[:, half:]
                else:
                    re = pltpu.roll(both[:, :half], half - r * kept, 1)
                    im = pltpu.roll(both[:, half:], half - r * kept, 1)
                for o in range(groups):
                    w_re = w_ref[0, i, o, r].astype(F32)
                    w_im = w_ref[1, i, o, r].astype(F32)
                    total[o][0] = total[o][0] + (re * w_re - im * w_im)
                    total[o][1] = total[o][1] + (re * w_im + im * w_re)
        for o in range(groups):
            out_ref[o] = jnp.concatenate(total[o], axis=1).astype(BF16)

    return call(
        kernel,
        (8 * groups * groups * chans * rows * half, 2 * placed.size),
        grid=(rows // step,),
        in_specs=[
            pl.BlockSpec((groups, step, lanes), lambda t: (0, t, 0)),
            pl.BlockSpec(placed.shape[:4] + (step, half), lambda t: (0, 0, 0, 0, t, 0)),
        ],
        out_specs=pl.BlockSpec((groups, step, lanes), lambda t: (0, t, 0)),
        out_shape=jax.ShapeDtypeStruct(spectra.shape, BF16),
        name="mix",
    )(spectra, placed)


def inverse_x(mixed, slabs, inv_two):
    groups, rows, lanes = mixed.shape
    two = inv_two.shape[1] // 2
    own = groups * rows // two
    half = lanes // 2

    def kernel(mixed_ref, table_ref, out_ref, wide, found):
        flat = mixed_ref[...].reshape(groups * rows, lanes).astype(F32)
        wide[0] = flat[:, :half]
        wide[1] = flat[:, half:]
        for n in range(own):
            pick = pl.ds(n, two, stride=own)
            modes = jnp.concatenate([wide[0, pick, :], wide[1, pick, :]], axis=1)
            twice = jnp.concatenate([modes, turn(modes)], axis=0).astype(BF16)
            planes = dot(table_ref[...], twice)
            put = pl.ds(n, NG, stride=own)
            found[0, put, :] = planes[:, :half]
            found[1, put, :] = planes[:, half:]
        both = jnp.concatenate([found[0], found[1]], axis=1)
        out_ref[...] = both.reshape(slabs, NG * own // slabs, lanes).astype(BF16)

    return call(
        kernel,
        (4 * own * two * NG * lanes, 4 * NG * own * lanes),
        in_specs=[pl.BlockSpec(memory_space=pltpu.VMEM)] * 2,
        out_specs=pl.BlockSpec(memory_space=pltpu.VMEM),
        out_shape=jax.ShapeDtypeStruct((slabs, NG * own // slabs, lanes), BF16),
        scratch_shapes=[
            pltpu.VMEM((2, two * own, half), F32),
            pltpu.VMEM((2, NG * own, half), F32),
        ],
        name="inverse_x",
    )(mixed, inv_two)


def inverse_yz(back_x, shift, sample, shape, filled, inv_two, inv_z):
    slabs, rows, lanes = back_x.shape
    _, chans, planes, _, _ = shape
    two = inv_two.shape[1] // 2
    own = two // slabs
    step = max(2, 16 // own)

    def kernel(back_ref, shift_ref, inv_two_ref, inv_z_ref, *refs):
        out_ref = refs[-1]
        wide = back_ref[...].astype(F32)
        for x in range(step):
            modes = wide[:, x * own : (x + 1) * own, :].reshape(two, lanes)
            twice = jnp.concatenate([modes, turn(modes)], axis=0).astype(BF16)
            back_y = dot(inv_two_ref[...], twice).astype(BF16)
            for c in range(chans):
                shifted = dot(back_y, inv_z_ref[c]) + shift_ref[c]
                half = 0.5 * shifted
                value = half + half * lax.erf(shifted * np.float32(np.sqrt(0.5)))
                out_ref[0, c, x] = value.astype(BF16)

    extra = [] if filled is None else [filled]
    return call(
        kernel,
        (2 * planes * NG * (2 * two * lanes + chans * lanes * NG), 2 * chans * planes * NG * NG),
        grid=(planes // step,),
        in_specs=[
            pl.BlockSpec((slabs, step * own, lanes), lambda i: (0, i, 0)),
            pl.BlockSpec(memory_space=pltpu.SMEM),
            pl.BlockSpec(inv_two.shape, lambda i: (0, 0)),
            pl.BlockSpec(inv_z.shape, lambda i: (0, 0, 0)),
        ]
        + [pl.BlockSpec(memory_space=pl.ANY)] * len(extra),
        out_specs=pl.BlockSpec((1, chans, step, NG, NG), lambda i: (sample, 0, i, 0, 0)),
        out_shape=jax.ShapeDtypeStruct(shape, BF16),
        input_output_aliases={} if filled is None else {4: 0},
        name="inverse_yz",
    )(back_x, shift, inv_two, inv_z, *extra)


def exchange(blocks, axis):
    return lax.all_to_all(blocks, axis, split_axis=0, concat_axis=0, tiled=True)


def on_device(slabs, groups, state, weights, shift):
    samples, chans = state.shape[:2]
    fwd_z, fwd_two, inv_two, inv_z = make_tables(chans)
    shift = shift.astype(F32)
    placed = place_weights(jnp.transpose(weights, (0, 1, 2, 4, 5, 3)), chans)
    out = None
    for b in range(samples):
        coef_y = exchange(forward_zy(state, b, slabs, fwd_z, fwd_two), "slab")
        spectra = exchange(forward_x(coef_y, groups, fwd_two), "chan")
        mixed = exchange(mix(spectra, placed, KM), "chan")
        back_x = exchange(inverse_x(mixed, slabs, inv_two), "slab")
        out = inverse_yz(back_x, shift, b, state.shape, out, inv_two, inv_z)
    return out


def solution(mesh):
    slabs, groups = mesh.shape["slab"], mesh.shape["chan"]
    return jax.shard_map(
        functools.partial(on_device, slabs, groups),
        mesh=mesh,
        in_specs=(
            P(None, "chan", "slab", None, None),
            P(None, None, "chan", None, None, "slab"),
            P("chan"),
        ),
        out_specs=P(None, "chan", "slab", None, None),
        check_vma=False,
    )
```

time: 572 us -> 209 us (0.37)
  matrix products: 219 us -> 0 us
  local copies, waits for them, and re-layouts: 214 us -> 6.1 us
  Pallas kernels: 0 us -> 94.2 us
  waiting for transfers between devices: 104 us -> 75.8 us
  starting transfers between devices: 18.3 us -> 31.7 us
  other arithmetic: 10.8 us -> 0.01 us
    dot_general x9 -> x0, matrix products: 219 us -> none  [the longest x1 154 us: on_device(): jnp.einsum('bcxkpy,kpz->bcxyz', back_y, inv_z, preferred_element_type=f32)]
    unnamed x16 -> x18, local copies, waits for them, and re-layouts: 107 us -> 6.1 us
    pallas_call x0 -> x11, Pallas kernels: none -> 94.2 us  [the longest x2 34.3 us: forward_zy(): call(kernel, (2 * planes * NG * lanes * (chans * NG + 2 * two), 2 * chans...]
    all_to_all x6 -> x0, local copies, waits for them, and re-layouts: 49 us -> none  [the longest x3 44 us: on_device(): lax.all_to_all(coef_y, 'slab', split_axis=5, concat_axis=2, tiled=True)]
    convert_element_type x3 -> x0, local copies, waits for them, and re-layouts: 33.6 us -> none  [the longest x1 18.5 us: on_device(): jnp.einsum('bcxkpy,pyqn->bcxkqn', coef_z, table_y, preferred_element_type...]
    all_to_all x4 -> x8, waiting for transfers between devices: 104 us -> 75.8 us  [exchange(): return lax.all_to_all(blocks, axis, split_axis=0, concat_axis=0, tiled=True)]
    all_to_all x4 -> x8, starting transfers between devices: 18.3 us -> 31.7 us  [exchange(): return lax.all_to_all(blocks, axis, split_axis=0, concat_axis=0, tiled=True)]
    slice x2 -> x0, local copies, waits for them, and re-layouts: 12.6 us -> none  [the longest x1 12 us: complex_mix(): wgt_re = wgt_part[..., 0, :]]
  transfers between devices with their start and end apart: 4 -> 8, of which waited for: 3 -> 6; matrix products, arithmetic and copies ran while one was open for 13% -> 0% of each run, Pallas kernels for 0% -> 29%
where the time goes in v1:
time: 209 us; the launch traced here: 208 us
  Pallas kernels  94.2 us (45%)
  waiting for transfers between devices  75.8 us (36%)
  starting transfers between devices  31.7 us (15%)
  local copies, waits for them, and re-layouts  6.1 us (3%)
    all_to_all x8, waiting for transfers between devices, exchange(): return lax.all_to_all(blocks, axis, split_axis=0, concat_axis=0, tiled=True)  75.8 us
    pallas_call x2, Pallas kernels, forward_zy(): call(kernel, (2 * planes * NG * lanes * (chans * NG + 2 * two), 2 * chans...  34.3 us
    pallas_call x2, Pallas kernels, inverse_yz(): call(kernel, (2 * planes * NG * (2 * two * lanes + chans * lanes * NG), 2...  32.7 us
    all_to_all x8, starting transfers between devices, exchange(): return lax.all_to_all(blocks, axis, split_axis=0, concat_axis=0, tiled=True)  31.7 us
    pallas_call x1, Pallas kernels, place_weights(): call(kernel, (2 * weights.size, 10 * weights.size), grid=(groups, outputs...  13.1 us
    pallas_call x2, Pallas kernels, mix(): call(kernel, (8 * groups * groups * chans * rows * half, 2 * placed.size)...  8.21 us
    unnamed x18, local copies, waits for them, and re-layouts  6.1 us
  transfers between devices with their start and end apart: 8, of which 6 were waited for; matrix products, arithmetic and copies ran while one was open for 0% of the time, Pallas kernels for 29%

profile of v1, /device:TPU:0, one launch (start us, length us, event | category | flops | bytes accessed | tf_op | source)
XLA Modules:
  0.0 208.0 jit_solution(4057787442869270147)
XLA Ops:
  0.0 0.0 copy-start.3
  0.0 1.0 copy-done.3
  1.0 0.0 copy-start.5
  1.0 0.8 copy-done.5
  1.9 0.0 copy-start.4
  1.9 0.0 copy-start.6
  1.9 17.1 %forward_zy.3 = bf16[8,256,256]{2,1,0:T(8,128)(2,1)} custom-call(bf16[2,4,32,256,256]{4,3,2,1,0:T(8,128)(2,1)} %state_ref.3, bf16[1024,256]{1,0:T(8,128)(2,1)S(1)} %copy-done.3, bf16[128,256]{1,0:T(8,128)(2,1)S(1)} %copy-done.5), custom_call_target="tpu_custom_call" | custom-call | flops 4831838208 | bytes 16777216 | tf_op jit(solution)/shard_map/forward_zy/pallas_call | solution.py:95
  19.0 7.3 %all-to-all-start.4 = ((bf16[8,256,256]{2,1,0:T(8,128)(2,1)}), bf16[8,256,256]{2,1,0:T(8,128)(2,1)S(1)}, u32[]{:S(2)}, u32[]{:S(2)}) async-start(bf16[8,256,256]{2,1,0:T(8,128)(2,1)} %forward_zy.3), calls=%async_computation.4 | async-start | bytes 2097152 | tf_op jit(solution)/shard_map/all_to_all | solution.py:289
  26.3 0.0 copy-done.4
  26.3 0.0 copy-done.6
  26.3 0.0 copy-start.7
  26.3 0.0 copy-start.8
  26.3 0.0 copy-start.2
  26.4 17.1 %forward_zy.2 = bf16[8,256,256]{2,1,0:T(8,128)(2,1)} custom-call(bf16[2,4,32,256,256]{4,3,2,1,0:T(8,128)(2,1)} %state_ref.3, bf16[1024,256]{1,0:T(8,128)(2,1)S(1)} %copy-done.4, bf16[128,256]{1,0:T(8,128)(2,1)S(1)} %copy-done.6), custom_call_target="tpu_custom_call" | custom-call | flops 4831838208 | bytes 16777216 | tf_op jit(solution)/shard_map/forward_zy/pallas_call | solution.py:95
  43.5 8.6 %all-to-all-done.4.coef_ref = bf16[8,256,256]{2,1,0:T(8,128)(2,1)S(1)} async-done(((bf16[8,256,256]{2,1,0:T(8,128)(2,1)}), bf16[8,256,256]{2,1,0:T(8,128)(2,1)S(1)}, u32[]{:S(2)}, u32[]{:S(2)}) %all-to-all-start.4) | async-done | bytes 1048608 | tf_op jit(solution)/shard_map/all_to_all | solution.py:289
  52.1 3.6 %all-to-all-start = ((bf16[8,256,256]{2,1,0:T(8,128)(2,1)}), bf16[8,256,256]{2,1,0:T(8,128)(2,1)S(1)}, u32[]{:S(2)}, u32[]{:S(2)}) async-start(bf16[8,256,256]{2,1,0:T(8,128)(2,1)} %forward_zy.2), calls=%async_computation | async-start | bytes 2097152 | tf_op jit(solution)/shard_map/all_to_all | solution.py:289
  55.7 1.3 forward_x.3
  57.0 24.6 %all-to-all-done.coef_ref = bf16[8,256,256]{2,1,0:T(8,128)(2,1)S(1)} async-done(((bf16[8,256,256]{2,1,0:T(8,128)(2,1)}), bf16[8,256,256]{2,1,0:T(8,128)(2,1)S(1)}, u32[]{:S(2)}, u32[]{:S(2)}) %all-to-all-start) | async-done | bytes 1048608 | tf_op jit(solution)/shard_map/all_to_all | solution.py:289
  81.6 3.4 %all-to-all-start.5 = ((bf16[4,128,256]{2,1,0:T(8,128)(2,1)}), bf16[4,128,256]{2,1,0:T(8,128)(2,1)S(1)}, u32[]{:S(2)}, u32[]{:S(2)}) async-start(bf16[4,128,256]{2,1,0:T(8,128)(2,1)} %forward_x.3), calls=%async_computation.5 | async-start | bytes 524288 | tf_op jit(solution)/shard_map/all_to_all | solution.py:289
  85.0 1.3 forward_x.2
  86.4 4.7 %all-to-all-done.5.spec_ref = bf16[4,128,256]{2,1,0:T(8,128)(2,1)S(1)} async-done(((bf16[4,128,256]{2,1,0:T(8,128)(2,1)}), bf16[4,128,256]{2,1,0:T(8,128)(2,1)S(1)}, u32[]{:S(2)}, u32[]{:S(2)}) %all-to-all-start.5) | async-done | bytes 262176 | tf_op jit(solution)/shard_map/all_to_all | solution.py:289
  91.0 3.4 %all-to-all-start.1 = ((bf16[4,128,256]{2,1,0:T(8,128)(2,1)}), bf16[4,128,256]{2,1,0:T(8,128)(2,1)S(1)}, u32[]{:S(2)}, u32[]{:S(2)}) async-start(bf16[4,128,256]{2,1,0:T(8,128)(2,1)} %forward_x.2), calls=%async_computation.1 | async-start | bytes 524288 | tf_op jit(solution)/shard_map/all_to_all | solution.py:289
  94.4 13.1 %place_weights.1.w_ref = bf16[2,4,4,4,128,128]{5,4,3,2,1,0:T(8,128)(2,1)S(1)} custom-call(bf16[16,16,16,2,8,32]{5,4,3,2,1,0:T(8,128)(2,1)} %bitcast.1), custom_call_target="tpu_custom_call" | custom-call | flops 4194304 | bytes 20971520 | tf_op jit(solution)/shard_map/place_weights/pallas_call | solution.py:161
  107.5 4.1 %mix.3 = bf16[4,128,256]{2,1,0:T(8,128)(2,1)} custom-call(bf16[4,128,256]{2,1,0:T(8,128)(2,1)S(1)} %all-to-all-done.5.spec_ref, bf16[2,4,4,4,128,128]{5,4,3,2,1,0:T(8,128)(2,1)S(1)} %place_weights.1.w_ref), custom_call_target="tpu_custom_call" | custom-call | flops 8388608 | bytes 4194304 | tf_op jit(solution)/shard_map/mix/pallas_call | solution.py:200
  111.6 0.0 copy-start
  111.6 2.0 copy-done
  113.7 0.0 all-to-all-done.1.spec_ref
  113.7 3.4 %all-to-all-start.6 = ((bf16[4,128,256]{2,1,0:T(8,128)(2,1)}), bf16[4,128,256]{2,1,0:T(8,128)(2,1)S(1)}, u32[]{:S(2)}, u32[]{:S(2)}) async-start(bf16[4,128,256]{2,1,0:T(8,128)(2,1)} %mix.3), calls=%async_computation.6 | async-start | bytes 524288 | tf_op jit(solution)/shard_map/all_to_all | solution.py:289
  117.1 0.0 copy-start.1
  117.1 2.2 %copy-done.1 = bf16[2,4,4,4,128,128]{5,4,3,2,1,0:T(8,128)(2,1)S(1)} copy-done((bf16[2,4,4,4,128,128]{5,4,3,2,1,0:T(8,128)(2,1)S(1)}, bf16[2,4,4,4,128,128]{5,4,3,2,1,0:T(8,128)(2,1)}, u32[]{:S(2)}) %copy-start.1) | copy-done | bytes 4194328
  119.3 4.1 %mix.2 = bf16[4,128,256]{2,1,0:T(8,128)(2,1)} custom-call(bf16[4,128,256]{2,1,0:T(8,128)(2,1)S(1)} %all-to-all-done.1.spec_ref, bf16[2,4,4,4,128,128]{5,4,3,2,1,0:T(8,128)(2,1)S(1)} %copy-done.1), custom_call_target="tpu_custom_call" | custom-call | flops 8388608 | bytes 4194304 | tf_op jit(solution)/shard_map/mix/pallas_call | solution.py:200
  123.4 0.0 all-to-all-done.6.mixed_ref
  123.4 3.4 %all-to-all-start.2 = ((bf16[4,128,256]{2,1,0:T(8,128)(2,1)}), bf16[4,128,256]{2,1,0:T(8,128)(2,1)S(1)}, u32[]{:S(2)}, u32[]{:S(2)}) async-start(bf16[4,128,256]{2,1,0:T(8,128)(2,1)} %mix.2), calls=%async_computation.2 | async-start | bytes 524288 | tf_op jit(solution)/shard_map/all_to_all | solution.py:289
  126.8 0.0 copy-done.7
  126.8 1.6 inverse_x.3
  128.4 4.3 %all-to-all-done.2.mixed_ref = bf16[4,128,256]{2,1,0:T(8,128)(2,1)S(1)} async-done(((bf16[4,128,256]{2,1,0:T(8,128)(2,1)}), bf16[4,128,256]{2,1,0:T(8,128)(2,1)S(1)}, u32[]{:S(2)}, u32[]{:S(2)}) %all-to-all-start.2) | async-done | bytes 262176 | tf_op jit(solution)/shard_map/all_to_all | solution.py:289
  132.8 3.6 %all-to-all-start.7 = ((bf16[8,256,256]{2,1,0:T(8,128)(2,1)}), bf16[8,256,256]{2,1,0:T(8,128)(2,1)S(1)}, u32[]{:S(2)}, u32[]{:S(2)}) async-start(bf16[8,256,256]{2,1,0:T(8,128)(2,1)} %inverse_x.3), calls=%async_computation.7 | async-start | bytes 2097152 | tf_op jit(solution)/shard_map/all_to_all | solution.py:289
  136.4 1.7 inverse_x.2
  138.1 24.0 %all-to-all-done.7.back_ref = bf16[8,256,256]{2,1,0:T(8,128)(2,1)S(1)} async-done(((bf16[8,256,256]{2,1,0:T(8,128)(2,1)}), bf16[8,256,256]{2,1,0:T(8,128)(2,1)S(1)}, u32[]{:S(2)}, u32[]{:S(2)}) %all-to-all-start.7) | async-done | bytes 1048608 | tf_op jit(solution)/shard_map/all_to_all | solution.py:289
  162.1 3.6 %all-to-all-start.3 = ((bf16[8,256,256]{2,1,0:T(8,128)(2,1)}), bf16[8,256,256]{2,1,0:T(8,128)(2,1)S(1)}, u32[]{:S(2)}, u32[]{:S(2)}) async-start(bf16[8,256,256]{2,1,0:T(8,128)(2,1)} %inverse_x.2), calls=%async_computation.3 | async-start | bytes 2097152 | tf_op jit(solution)/shard_map/all_to_all | solution.py:289
  165.7 0.0 copy-done.8
  165.7 0.0 copy-done.2
  165.7 16.4 %inverse_yz.2.refs_0_ = bf16[2,4,32,256,256]{4,3,2,1,0:T(8,128)(2,1)} custom-call(bf16[8,256,256]{2,1,0:T(8,128)(2,1)S(1)} %all-to-all-done.7.back_ref, f32[4]{0:T(128)S(1)} %convert_element_type.3.shift_ref, bf16[256,128]{1,0:T(8,128)(2,1)S(1)} %copy-done.7, bf16[4,256,256]{2,1,0:T(8,128)(2,1)S(1)} %copy-done.2), custom_call_target="tpu_custom_call" | custom-call | flops 4831838208 | bytes 16777216 | tf_op jit(solution)/shard_map/inverse_yz/pallas_call | solution.py:270
  182.1 9.6 %all-to-all-done.3.back_ref = bf16[8,256,256]{2,1,0:T(8,128)(2,1)S(1)} async-done(((bf16[8,256,256]{2,1,0:T(8,128)(2,1)}), bf16[8,256,256]{2,1,0:T(8,128)(2,1)S(1)}, u32[]{:S(2)}, u32[]{:S(2)}) %all-to-all-start.3) | async-done | bytes 1048608 | tf_op jit(solution)/shard_map/all_to_all | solution.py:289
  191.6 16.3 %inverse_yz.3 = bf16[2,4,32,256,256]{4,3,2,1,0:T(8,128)(2,1)} custom-call(bf16[8,256,256]{2,1,0:T(8,128)(2,1)S(1)} %all-to-all-done.3.back_ref, f32[4]{0:T(128)S(1)} %convert_element_type.3.shift_ref, bf16[256,128]{1,0:T(8,128)(2,1)S(1)} %copy-done.7, bf16[4,256,256]{2,1,0:T(8,128)(2,1)S(1)} %copy-done.2, ...), custom_call_target="tpu_custom_call", output_to_operand_aliasing={{}: (4, {})} | custom-call | flops 4831838208 | bytes 16777216 | tf_op jit(solution)/shard_map/inverse_yz/pallas_call | solution.py:270
  (1 shorter events, 0.0 us)
Async XLA Ops:
  0.0 1.0 copy-start.3
  1.0 0.8 copy-start.5
  1.9 24.4 %copy-start.4 = (bf16[1024,256]{1,0:T(8,128)(2,1)S(1)}, bf16[1024,256]{1,0:T(8,128)(2,1)}, u32[]{:S(2)}) copy-start(bf16[1024,256]{1,0:T(8,128)(2,1)} %constant.8.clone.fwd_z_ref) | copy-start | bytes 1572868
  1.9 24.4 %copy-start.6 = (bf16[128,256]{1,0:T(8,128)(2,1)S(1)}, bf16[128,256]{1,0:T(8,128)(2,1)}, u32[]{:S(2)}) copy-start(bf16[128,256]{1,0:T(8,128)(2,1)} %constant.9.clone.fwd_two_ref.table_ref) | copy-start | bytes 196612
  19.0 33.0 %all-to-all-start.4 = ((bf16[8,256,256]{2,1,0:T(8,128)(2,1)}), bf16[8,256,256]{2,1,0:T(8,128)(2,1)S(1)}, u32[]{:S(2)}, u32[]{:S(2)}) async-start(bf16[8,256,256]{2,1,0:T(8,128)(2,1)} %forward_zy.3), calls=%async_computation.4 | async-start | bytes 2097152 | tf_op jit(solution)/shard_map/all_to_all | solution.py:289
  26.3 100.5 %copy-start.7 = (bf16[256,128]{1,0:T(8,128)(2,1)S(1)}, bf16[256,128]{1,0:T(8,128)(2,1)}, u32[]{:S(2)}) copy-start(bf16[256,128]{1,0:T(8,128)(2,1)} %constant.10.clone.table_ref.inv_two_ref) | copy-start | bytes 196612
  26.3 139.4 %copy-start.8 = (bf16[4]{0:T(256)(128)(2,1)S(1)}, bf16[4]{0:T(256)(128)(2,1)}, u32[]{:S(2)}) copy-start(bf16[4]{0:T(256)(128)(2,1)} %param.9) | copy-start | bytes 28
  26.3 139.4 %copy-start.2 = (bf16[4,256,256]{2,1,0:T(8,128)(2,1)S(1)}, bf16[4,256,256]{2,1,0:T(8,128)(2,1)}, u32[]{:S(2)}) copy-start(bf16[4,256,256]{2,1,0:T(8,128)(2,1)} %constant.11.clone.inv_z_ref) | copy-start | bytes 1572868
  52.1 29.5 %all-to-all-start = ((bf16[8,256,256]{2,1,0:T(8,128)(2,1)}), bf16[8,256,256]{2,1,0:T(8,128)(2,1)S(1)}, u32[]{:S(2)}, u32[]{:S(2)}) async-start(bf16[8,256,256]{2,1,0:T(8,128)(2,1)} %forward_zy.2), calls=%async_computation | async-start | bytes 2097152 | tf_op jit(solution)/shard_map/all_to_all | solution.py:289
  81.6 9.4 %all-to-all-start.5 = ((bf16[4,128,256]{2,1,0:T(8,128)(2,1)}), bf16[4,128,256]{2,1,0:T(8,128)(2,1)S(1)}, u32[]{:S(2)}, u32[]{:S(2)}) async-start(bf16[4,128,256]{2,1,0:T(8,128)(2,1)} %forward_x.3), calls=%async_computation.5 | async-start | bytes 524288 | tf_op jit(solution)/shard_map/all_to_all | solution.py:289
  91.0 22.6 %all-to-all-start.1 = ((bf16[4,128,256]{2,1,0:T(8,128)(2,1)}), bf16[4,128,256]{2,1,0:T(8,128)(2,1)S(1)}, u32[]{:S(2)}, u32[]{:S(2)}) async-start(bf16[4,128,256]{2,1,0:T(8,128)(2,1)} %forward_x.2), calls=%async_computation.1 | async-start | bytes 524288 | tf_op jit(solution)/shard_map/all_to_all | solution.py:289
  111.6 2.0 copy-start
  113.7 9.7 %all-to-all-start.6 = ((bf16[4,128,256]{2,1,0:T(8,128)(2,1)}), bf16[4,128,256]{2,1,0:T(8,128)(2,1)S(1)}, u32[]{:S(2)}, u32[]{:S(2)}) async-start(bf16[4,128,256]{2,1,0:T(8,128)(2,1)} %mix.3), calls=%async_computation.6 | async-start | bytes 524288 | tf_op jit(solution)/shard_map/all_to_all | solution.py:289
  117.1 2.2 %copy-start.1 = (bf16[2,4,4,4,128,128]{5,4,3,2,1,0:T(8,128)(2,1)S(1)}, bf16[2,4,4,4,128,128]{5,4,3,2,1,0:T(8,128)(2,1)}, u32[]{:S(2)}) copy-start(bf16[2,4,4,4,128,128]{5,4,3,2,1,0:T(8,128)(2,1)} %copy-done) | copy-start | bytes 12582916
  123.4 9.4 %all-to-all-start.2 = ((bf16[4,128,256]{2,1,0:T(8,128)(2,1)}), bf16[4,128,256]{2,1,0:T(8,128)(2,1)S(1)}, u32[]{:S(2)}, u32[]{:S(2)}) async-start(bf16[4,128,256]{2,1,0:T(8,128)(2,1)} %mix.2), calls=%async_computation.2 | async-start | bytes 524288 | tf_op jit(solution)/shard_map/all_to_all | solution.py:289
  132.8 29.3 %all-to-all-start.7 = ((bf16[8,256,256]{2,1,0:T(8,128)(2,1)}), bf16[8,256,256]{2,1,0:T(8,128)(2,1)S(1)}, u32[]{:S(2)}, u32[]{:S(2)}) async-start(bf16[8,256,256]{2,1,0:T(8,128)(2,1)} %inverse_x.3), calls=%async_computation.7 | async-start | bytes 2097152 | tf_op jit(solution)/shard_map/all_to_all | solution.py:289
  162.1 29.5 %all-to-all-start.3 = ((bf16[8,256,256]{2,1,0:T(8,128)(2,1)}), bf16[8,256,256]{2,1,0:T(8,128)(2,1)S(1)}, u32[]{:S(2)}, u32[]{:S(2)}) async-start(bf16[8,256,256]{2,1,0:T(8,128)(2,1)} %inverse_x.2), calls=%async_computation.3 | async-start | bytes 2097152 | tf_op jit(solution)/shard_map/all_to_all | solution.py:289

commit v2 on v1

--- a/solution.py
+++ b/solution.py
@@ -81,14 +81,16 @@
     two = fwd_two.shape[0] // 2
     own = two // slabs
     lanes = fwd_z.shape[1]
-    step = max(4, 16 // own)
-
-    def kernel(state_ref, fwd_z_ref, fwd_two_ref, out_ref):
+    step = min(planes, max(8, 16 // own))
+
+    def kernel(state_ref, fwd_z_ref, fwd_two_ref, out_ref, coef_z):
+        for x in range(step):
+            plane = jnp.concatenate([state_ref[0, c, x] for c in range(chans)], axis=1)
+            coef_z[x] = dot(plane, fwd_z_ref[...]).astype(BF16)
         found = []
         for x in range(step):
-            plane = jnp.concatenate([state_ref[0, c, x] for c in range(chans)], axis=1)
-            coef_z = dot(plane, fwd_z_ref[...]).astype(BF16)
-            found.append(unturn(dot(fwd_two_ref[...], coef_z)).reshape(slabs, own, lanes))
+            modes = unturn(dot(fwd_two_ref[...], coef_z[x]))
+            found.append(modes.reshape(slabs, own, lanes))
         rows = jnp.stack(found, axis=1).reshape(slabs, step * own, lanes)
         out_ref[...] = rows.astype(BF16)
 
@@ -103,18 +105,20 @@
         ],
         out_specs=pl.BlockSpec((slabs, step * own, lanes), lambda i: (0, i, 0)),
         out_shape=jax.ShapeDtypeStruct((slabs, planes * own, lanes), BF16),
+        scratch_shapes=[pltpu.VMEM((step, NG, lanes), BF16)],
         name="forward_zy",
     )(state, fwd_z, fwd_two)
 
 
-def forward_x(coef_y, groups, fwd_two):
+def forward_x(coef_y, me, groups, fwd_two):
     slabs, rows, lanes = coef_y.shape
     two = fwd_two.shape[0] // 2
     own = two // slabs
     half = lanes // 2
     part = two // groups
 
-    def kernel(coef_ref, table_ref, out_ref, wide, found):
+    def kernel(me_ref, coef_ref, table_ref, *refs):
+        wide, found = refs[groups:]
         flat = coef_ref[...].reshape(slabs * rows, lanes).astype(F32)
         wide[0] = flat[:, :half]
         wide[1] = flat[:, half:]
@@ -125,30 +129,34 @@
             put = pl.ds(n, two, stride=own)
             found[0, put, :] = modes[:, :half]
             found[1, put, :] = modes[:, half:]
-        both = jnp.concatenate([found[0], found[1]], axis=1)
-        out_ref[...] = both.reshape(groups, part * own, lanes).astype(BF16)
+        for r in range(groups):
+            start = pl.multiple_of((me_ref[0] ^ r) * part * own, part * own)
+            pick = pl.ds(start, part * own)
+            both = jnp.concatenate([found[0, pick, :], found[1, pick, :]], axis=1)
+            refs[r][...] = both.astype(BF16)
 
     return call(
         kernel,
         (4 * own * two * NG * lanes, 4 * slabs * rows * lanes),
-        in_specs=[pl.BlockSpec(memory_space=pltpu.VMEM)] * 2,
-        out_specs=pl.BlockSpec(memory_space=pltpu.VMEM),
-        out_shape=jax.ShapeDtypeStruct((groups, part * own, lanes), BF16),
+        in_specs=[pl.BlockSpec(memory_space=pltpu.SMEM)]
+        + [pl.BlockSpec(memory_space=pltpu.VMEM)] * 2,
+        out_specs=[pl.BlockSpec(memory_space=pltpu.VMEM)] * groups,
+        out_shape=[jax.ShapeDtypeStruct((part * own, lanes), BF16)] * groups,
         scratch_shapes=[
             pltpu.VMEM((2, slabs * rows, half), F32),
             pltpu.VMEM((2, two * own, half), F32),
         ],
         name="forward_x",
-    )(coef_y, fwd_two)
-
-
-def place_weights(weights, chans):
+    )(me, coef_y, fwd_two)
+
+
+def place_weights(weights, me, chans):
     inputs, outputs, modes, _, own, kept = weights.shape
     groups = inputs // chans
     rows = modes * own
     lanes = chans * kept
 
-    def kernel(w_ref, out_ref):
+    def kernel(me_ref, w_ref, out_ref):
         for q in range(2):
             tiles = {}
             for i in range(chans):
@@ -161,28 +169,37 @@
     return call(
         kernel,
         (2 * weights.size, 10 * weights.size),
-        grid=(groups, outputs // chans),
-        in_specs=[
-            pl.BlockSpec((chans, chans, modes, 2, own, kept), lambda i, o: (i, o, 0, 0, 0, 0))
-        ],
-        out_specs=pl.BlockSpec((2, 1, 1, chans, rows, lanes), lambda i, o: (0, i, o, 0, 0, 0)),
+        grid_spec=pltpu.PrefetchScalarGridSpec(
+            num_scalar_prefetch=1,
+            grid=(groups, outputs // chans),
+            in_specs=[
+                pl.BlockSpec(
+                    (chans, chans, modes, 2, own, kept),
+                    lambda i, o, me_ref: (me_ref[0] ^ i, me_ref[0] ^ o, 0, 0, 0, 0),
+                )
+            ],
+            out_specs=pl.BlockSpec(
+                (2, 1, 1, chans, rows, lanes), lambda i, o, me_ref: (0, i, o, 0, 0, 0)
+            ),
+        ),
         out_shape=jax.ShapeDtypeStruct(
             (2, groups, outputs // chans, chans, rows, lanes), BF16
         ),
         name="place_weights",
-    )(weights)
+    )(me, weights)
 
 
 def mix(spectra, placed, kept):
-    groups, rows, lanes = spectra.shape
+    groups = len(spectra)
+    rows, lanes = spectra[0].shape
     half = lanes // 2
     chans = placed.shape[3]
-    step = 16
-
-    def kernel(spec_ref, w_ref, out_ref):
+    step = min(rows, 32)
+
+    def kernel(w_ref, *refs):
         total = [[jnp.zeros((step, half), F32) for _ in range(2)] for _ in range(groups)]
         for i in range(groups):
-            both = spec_ref[i].astype(F32)
+            both = refs[i][...].astype(F32)
             for r in range(chans):
                 if r == 0:
                     re, im = both[:, :half], both[:, half:]
@@ -195,32 +212,34 @@
                     total[o][0] = total[o][0] + (re * w_re - im * w_im)
                     total[o][1] = total[o][1] + (re * w_im + im * w_re)
         for o in range(groups):
-            out_ref[o] = jnp.concatenate(total[o], axis=1).astype(BF16)
+            refs[groups + o][...] = jnp.concatenate(total[o], axis=1).astype(BF16)
 
     return call(
         kernel,
         (8 * groups * groups * chans * rows * half, 2 * placed.size),
         grid=(rows // step,),
-        in_specs=[
-            pl.BlockSpec((groups, step, lanes), lambda t: (0, t, 0)),
-            pl.BlockSpec(placed.shape[:4] + (step, half), lambda t: (0, 0, 0, 0, t, 0)),
-        ],
-        out_specs=pl.BlockSpec((groups, step, lanes), lambda t: (0, t, 0)),
-        out_shape=jax.ShapeDtypeStruct(spectra.shape, BF16),
+        in_specs=[pl.BlockSpec(placed.shape[:4] + (step, half), lambda t: (0, 0, 0, 0, t, 0))]
+        + [pl.BlockSpec((step, lanes), lambda t: (t, 0))] * groups,
+        out_specs=[pl.BlockSpec((step, lanes), lambda t: (t, 0))] * groups,
+        out_shape=[jax.ShapeDtypeStruct((rows, lanes), BF16)] * groups,
         name="mix",
-    )(spectra, placed)
-
-
-def inverse_x(mixed, slabs, inv_two):
-    groups, rows, lanes = mixed.shape
+    )(placed, *spectra)
+
+
+def inverse_x(mixed, me, slabs, inv_two):
+    groups = len(mixed)
+    rows, lanes = mixed[0].shape
     two = inv_two.shape[1] // 2
     own = groups * rows // two
     half = lanes // 2
 
-    def kernel(mixed_ref, table_ref, out_ref, wide, found):
-        flat = mixed_ref[...].reshape(groups * rows, lanes).astype(F32)
-        wide[0] = flat[:, :half]
-        wide[1] = flat[:, half:]
+    def kernel(me_ref, table_ref, *refs):
+        out_ref, wide, found = refs[groups:]
+        for r in range(groups):
+            put = pl.ds(pl.multiple_of((me_ref[0] ^ r) * rows, rows), rows)
+            both = refs[r][...].astype(F32)
+            wide[0, put, :] = both[:, :half]
+            wide[1, put, :] = both[:, half:]
         for n in range(own):
             pick = pl.ds(n, two, stride=own)
             modes = jnp.concatenate([wide[0, pick, :], wide[1, pick, :]], axis=1)
@@ -235,7 +254,8 @@
     return call(
         kernel,
         (4 * own * two * NG * lanes, 4 * NG * own * lanes),
-        in_specs=[pl.BlockSpec(memory_space=pltpu.VMEM)] * 2,
+        in_specs=[pl.BlockSpec(memory_space=pltpu.SMEM)]
+        + [pl.BlockSpec(memory_space=pltpu.VMEM)] * (1 + groups),
         out_specs=pl.BlockSpec(memory_space=pltpu.VMEM),
         out_shape=jax.ShapeDtypeStruct((slabs, NG * own // slabs, lanes), BF16),
         scratch_shapes=[
@@ -243,7 +263,7 @@
             pltpu.VMEM((2, NG * own, half), F32),
         ],
         name="inverse_x",
-    )(mixed, inv_two)
+    )(me, inv_two, *mixed)
 
 
 def inverse_yz(back_x, shift, sample, shape, filled, inv_two, inv_z):
@@ -251,20 +271,21 @@
     _, chans, planes, _, _ = shape
     two = inv_two.shape[1] // 2
     own = two // slabs
-    step = max(2, 16 // own)
+    step = min(planes, max(8, 16 // own))
 
     def kernel(back_ref, shift_ref, inv_two_ref, inv_z_ref, *refs):
-        out_ref = refs[-1]
+        out_ref, back_y = refs[-2:]
         wide = back_ref[...].astype(F32)
         for x in range(step):
             modes = wide[:, x * own : (x + 1) * own, :].reshape(two, lanes)
             twice = jnp.concatenate([modes, turn(modes)], axis=0).astype(BF16)
-            back_y = dot(inv_two_ref[...], twice).astype(BF16)
-            for c in range(chans):
-                shifted = dot(back_y, inv_z_ref[c]) + shift_ref[c]
-                half = 0.5 * shifted
-                value = half + half * lax.erf(shifted * np.float32(np.sqrt(0.5)))
-                out_ref[0, c, x] = value.astype(BF16)
+            back_y[x] = dot(inv_two_ref[...], twice).astype(BF16)
+        flat = back_y[...].reshape(step * NG, lanes)
+        for c in range(chans):
+            shifted = dot(flat, inv_z_ref[c]) + shift_ref[c]
+            half = 0.5 * shifted
+            value = half + half * lax.erf(shifted * np.float32(np.sqrt(0.5)))
+            out_ref[0, c] = value.astype(BF16).reshape(step, NG, NG)
 
     extra = [] if filled is None else [filled]
     return call(
@@ -280,6 +301,7 @@
         + [pl.BlockSpec(memory_space=pl.ANY)] * len(extra),
         out_specs=pl.BlockSpec((1, chans, step, NG, NG), lambda i: (sample, 0, i, 0, 0)),
         out_shape=jax.ShapeDtypeStruct(shape, BF16),
+        scratch_shapes=[pltpu.VMEM((step, NG, lanes), BF16)],
         input_output_aliases={} if filled is None else {4: 0},
         name="inverse_yz",
     )(back_x, shift, inv_two, inv_z, *extra)
@@ -287,20 +309,33 @@
 
 def exchange(blocks, axis):
     return lax.all_to_all(blocks, axis, split_axis=0, concat_axis=0, tiled=True)
+
+
+def swap(blocks, axis):
+    count = len(blocks)
+    return list(blocks[:1]) + [
+        lax.ppermute(blocks[r], axis, [(i, i ^ r) for i in range(count)]) for r in range(1, count)
+    ]
 
 
 def on_device(slabs, groups, state, weights, shift):
     samples, chans = state.shape[:2]
     fwd_z, fwd_two, inv_two, inv_z = make_tables(chans)
     shift = shift.astype(F32)
-    placed = place_weights(jnp.transpose(weights, (0, 1, 2, 4, 5, 3)), chans)
+    me = lax.axis_index("chan").reshape(1)
+    placed = place_weights(jnp.transpose(weights, (0, 1, 2, 4, 5, 3)), me, chans)
+    coef_y = [
+        exchange(forward_zy(state, b, slabs, fwd_z, fwd_two), "slab") for b in range(samples)
+    ]
+    coef_y[0], placed = lax.optimization_barrier((coef_y[0], placed))
+    back_x = []
+    for b in range(samples):
+        spectra = swap(forward_x(coef_y[b], me, groups, fwd_two), "chan")
+        mixed = swap(mix(spectra, placed, KM), "chan")
+        back_x.append(exchange(inverse_x(mixed, me, slabs, inv_two), "slab"))
     out = None
     for b in range(samples):
-        coef_y = exchange(forward_zy(state, b, slabs, fwd_z, fwd_two), "slab")
-        spectra = exchange(forward_x(coef_y, groups, fwd_two), "chan")
-        mixed = exchange(mix(spectra, placed, KM), "chan")
-        back_x = exchange(inverse_x(mixed, slabs, inv_two), "slab")
-        out = inverse_yz(back_x, shift, b, state.shape, out, inv_two, inv_z)
+        out = inverse_yz(back_x[b], shift, b, state.shape, out, inv_two, inv_z)
     return out
 
 

time: 209 us -> 154 us (0.74)
  Pallas kernels: 94.2 us -> 65.5 us
  waiting for transfers between devices: 75.8 us -> 53.3 us
  starting transfers between devices: 31.7 us -> 28.4 us
    all_to_all x8 -> x4, waiting for transfers between devices: 75.8 us -> 37.9 us  [exchange(): return lax.all_to_all(blocks, axis, split_axis=0, concat_axis=0, tiled=True)]
    ppermute x0 -> x12, waiting for transfers between devices: none -> 15.4 us  [swap(): lax.ppermute(blocks[r], axis, [(i, i ^ r) for i in range(count)])]
    pallas_call x2, Pallas kernels: 34.3 us -> 19.4 us  [forward_zy(): call(kernel, (2 * planes * NG * lanes * (chans * NG + 2 * two), 2 * chans...]
    all_to_all x8 -> x4, starting transfers between devices: 31.7 us -> 20.7 us  [exchange(): return lax.all_to_all(blocks, axis, split_axis=0, concat_axis=0, tiled=True)]
    pallas_call x2, Pallas kernels: 32.7 us -> 23.9 us  [inverse_yz(): call(kernel, (2 * planes * NG * (2 * two * lanes + chans * lanes * NG), 2...]
    ppermute x0 -> x12, starting transfers between devices: none -> 7.71 us  [swap(): lax.ppermute(blocks[r], axis, [(i, i ^ r) for i in range(count)])]
    pallas_call x2, Pallas kernels: 8.21 us -> 4.38 us  [mix(): call(kernel, (8 * groups * groups * chans * rows * half, 2 * placed.size)...]
  transfers between devices with their start and end apart: 8 -> 16, of which waited for: 6 -> 11; matrix products, arithmetic and copies ran while one was open for 0% -> 0% of each run, Pallas kernels for 29% -> 29%
where the time goes in v2:
time: 154 us; the launch traced here: 153 us
  Pallas kernels  65.5 us (43%)
  waiting for transfers between devices  53.3 us (35%)
  starting transfers between devices  28.4 us (18%)
  local copies, waits for them, and re-layouts  6.1 us (4%)
    all_to_all x4, waiting for transfers between devices, exchange(): return lax.all_to_all(blocks, axis, split_axis=0, concat_axis=0, tiled=True)  37.9 us
    pallas_call x2, Pallas kernels, inverse_yz(): call(kernel, (2 * planes * NG * (2 * two * lanes + chans * lanes * NG), 2...  23.9 us
    all_to_all x4, starting transfers between devices, exchange(): return lax.all_to_all(blocks, axis, split_axis=0, concat_axis=0, tiled=True)  20.7 us
    pallas_call x2, Pallas kernels, forward_zy(): call(kernel, (2 * planes * NG * lanes * (chans * NG + 2 * two), 2 * chans...  19.4 us
    ppermute x12, waiting for transfers between devices, swap(): lax.ppermute(blocks[r], axis, [(i, i ^ r) for i in range(count)])  15.4 us
    pallas_call x1, Pallas kernels, place_weights(): call(kernel, (2 * weights.size, 10 * weights.size), grid_spec=pltpu.Prefe...  13.1 us
    ppermute x12, starting transfers between devices, swap(): lax.ppermute(blocks[r], axis, [(i, i ^ r) for i in range(count)])  7.71 us
    unnamed x18, local copies, waits for them, and re-layouts  6.1 us
  transfers between devices with their start and end apart: 16, of which 11 were waited for; matrix products, arithmetic and copies ran while one was open for 0% of the time, Pallas kernels for 29%

profile of v2, /device:TPU:0, one launch (start us, length us, event | category | flops | bytes accessed | tf_op | source)
XLA Modules:
  0.0 153.4 jit_solution(17525332146417322640)
XLA Ops:
  0.0 0.0 copy-start.3
  0.0 1.0 copy-done.3
  1.0 0.0 copy-start.5
  1.0 0.8 copy-done.5
  1.9 0.0 copy-start.4
  1.9 0.0 copy-start.6
  1.9 9.7 %forward_zy.2 = bf16[8,256,256]{2,1,0:T(8,128)(2,1)} custom-call(bf16[2,4,32,256,256]{4,3,2,1,0:T(8,128)(2,1)} %state_ref.3, bf16[1024,256]{1,0:T(8,128)(2,1)S(1)} %copy-done.3, bf16[128,256]{1,0:T(8,128)(2,1)S(1)} %copy-done.5), custom_call_target="tpu_custom_call" | custom-call | flops 4831838208 | bytes 16777216 | tf_op jit(solution)/shard_map/forward_zy/pallas_call | solution.py:97
  11.6 0.0 copy-start.7
  11.6 7.4 %all-to-all-start = ((bf16[8,256,256]{2,1,0:T(8,128)(2,1)}), bf16[8,256,256]{2,1,0:T(8,128)(2,1)S(1)}, u32[]{:S(2)}, u32[]{:S(2)}) async-start(bf16[8,256,256]{2,1,0:T(8,128)(2,1)} %forward_zy.2), calls=%async_computation | async-start | bytes 2097152 | tf_op jit(solution)/shard_map/all_to_all | solution.py:311
  19.0 0.0 copy-done.4
  19.0 0.0 copy-done.6
  19.0 0.0 copy-start.8
  19.0 0.0 copy-start.2
  19.0 9.7 %forward_zy.3 = bf16[8,256,256]{2,1,0:T(8,128)(2,1)} custom-call(bf16[2,4,32,256,256]{4,3,2,1,0:T(8,128)(2,1)} %state_ref.3, bf16[1024,256]{1,0:T(8,128)(2,1)S(1)} %copy-done.4, bf16[128,256]{1,0:T(8,128)(2,1)S(1)} %copy-done.6), custom_call_target="tpu_custom_call" | custom-call | flops 4831838208 | bytes 16777216 | tf_op jit(solution)/shard_map/forward_zy/pallas_call | solution.py:97
  28.8 16.0 %all-to-all-done.coef_ref = bf16[8,256,256]{2,1,0:T(8,128)(2,1)S(1)} async-done(((bf16[8,256,256]{2,1,0:T(8,128)(2,1)}), bf16[8,256,256]{2,1,0:T(8,128)(2,1)S(1)}, u32[]{:S(2)}, u32[]{:S(2)}) %all-to-all-start) | async-done | bytes 1048608 | tf_op jit(solution)/shard_map/all_to_all | solution.py:311
  44.8 3.6 %all-to-all-start.1 = ((bf16[8,256,256]{2,1,0:T(8,128)(2,1)}), bf16[8,256,256]{2,1,0:T(8,128)(2,1)S(1)}, u32[]{:S(2)}, u32[]{:S(2)}) async-start(bf16[8,256,256]{2,1,0:T(8,128)(2,1)} %forward_zy.3), calls=%async_computation.1 | async-start | bytes 2097152 | tf_op jit(solution)/shard_map/all_to_all | solution.py:311
  48.4 13.1 %place_weights.1.w_ref = bf16[2,4,4,4,128,128]{5,4,3,2,1,0:T(8,128)(2,1)S(1)} custom-call(s32[1]{0:T(128)} %bitcast.me_ref, bf16[16,16,16,2,8,32]{5,4,3,2,1,0:T(8,128)(2,1)} %bitcast.2), custom_call_target="tpu_custom_call" | custom-call | flops 4194304 | bytes 20971520 | tf_op jit(solution)/shard_map/place_weights/pallas_call | solution.py:169
  61.5 0.6 forward_x.3
  62.1 0.1 collective-permute-start.6
  62.2 1.6 %collective-permute-start.7 = (bf16[128,256]{1,0:T(8,128)(2,1)S(1)}, bf16[128,256]{1,0:T(8,128)(2,1)S(1)}, u32[]{:S(2)}, u32[]{:S(2)}) collective-permute-start(bf16[128,256]{1,0:T(8,128)(2,1)S(1)} %get-tuple-element.35), channel_id=1, source_target_pairs={{0,2},{1,3},{2,0},{3,1},{4,6},{5,7},{6,4},{7,5},{8,10},{9,11},{10,... | collective-permute-start | bytes 196616 | tf_op jit(solution)/shard_map/ppermute | solution.py:317
  63.8 0.3 collective-permute-start.8
  64.1 0.0 collective-permute-done.6.refs_1_
  64.1 2.6 %collective-permute-done.7.refs_2_ = bf16[128,256]{1,0:T(8,128)(2,1)S(1)} collective-permute-done((bf16[128,256]{1,0:T(8,128)(2,1)S(1)}, bf16[128,256]{1,0:T(8,128)(2,1)S(1)}, u32[]{:S(2)}, u32[]{:S(2)}) %collective-permute-start.7) | collective-permute-done | bytes 65568 | tf_op jit(solution)/shard_map/ppermute | solution.py:317
  66.7 1.1 collective-permute-done.8.refs_3_
  67.8 2.2 %mix.3 = (bf16[128,256]{1,0:T(8,128)(2,1)S(1)}, bf16[128,256]{1,0:T(8,128)(2,1)S(1)}, bf16[128,256]{1,0:T(8,128)(2,1)S(1)}, bf16[128,256]{1,0:T(8,128)(2,1)S(1)}) custom-call(bf16[2,4,4,4,128,128]{5,4,3,2,1,0:T(8,128)(2,1)S(1)} %place_weights.1.w_ref, bf16[128,256]{1,0:T(8,128)(2,1)S(1)} %get-tuple-element.33.refs_0_, ...), custom_call_target="tpu_custom_call" | custom-call | flops 8388608 | bytes 4194304 | tf_op jit(solution)/shard_map/mix/pallas_call | solution.py:217
  70.0 0.0 copy-start
  70.0 2.0 %copy-done = bf16[2,4,4,4,128,128]{5,4,3,2,1,0:T(8,128)(2,1)} copy-done((bf16[2,4,4,4,128,128]{5,4,3,2,1,0:T(8,128)(2,1)}, bf16[2,4,4,4,128,128]{5,4,3,2,1,0:T(8,128)(2,1)S(1)}, u32[]{:S(2)}) %copy-start) | copy-done | bytes 4194328
  72.0 0.5 collective-permute-start.9
  72.5 1.5 collective-permute-start.10
  73.9 0.0 collective-permute-start.11
  73.9 0.0 collective-permute-done.9.refs_1_
  73.9 2.8 %collective-permute-done.10.refs_2_ = bf16[128,256]{1,0:T(8,128)(2,1)S(1)} collective-permute-done((bf16[128,256]{1,0:T(8,128)(2,1)S(1)}, bf16[128,256]{1,0:T(8,128)(2,1)S(1)}, u32[]{:S(2)}, u32[]{:S(2)}) %collective-permute-start.10) | collective-permute-done | bytes 65568 | tf_op jit(solution)/shard_map/ppermute | solution.py:317
  76.8 1.5 collective-permute-done.11.refs_3_
  78.2 0.0 copy-done.7
  78.2 1.7 %inverse_x.3 = bf16[8,256,256]{2,1,0:T(8,128)(2,1)} custom-call(s32[1]{0:T(128)} %bitcast.me_ref, bf16[256,128]{1,0:T(8,128)(2,1)S(1)} %copy-done.7, bf16[128,256]{1,0:T(8,128)(2,1)S(1)} %get-tuple-element.37.refs_0_, bf16[128,256]{1,0:T(8,128)(2,1)S(1)} %collective-permute-done.9.refs_1_, bf16[128,256]{1,0:T(8,128)(2,1)S(1)} %collective-permute-done.10.refs_2_, ...), custom_call_target="tpu_custom_call" | custom-call | flops 134217728 | bytes 2097152 | tf_op jit(solution)/shard_map/inverse_x/pallas_call | solution.py:254
  79.9 0.0 all-to-all-done.1.coef_ref
  79.9 6.0 %all-to-all-start.3 = ((bf16[8,256,256]{2,1,0:T(8,128)(2,1)}), bf16[8,256,256]{2,1,0:T(8,128)(2,1)S(1)}, u32[]{:S(2)}, u32[]{:S(2)}) async-start(bf16[8,256,256]{2,1,0:T(8,128)(2,1)} %inverse_x.3), calls=%async_computation.3 | async-start | bytes 2097152 | tf_op jit(solution)/shard_map/all_to_all | solution.py:311
  85.9 0.6 forward_x.2
  86.5 0.1 collective-permute-start
  86.6 0.9 collective-permute-start.1
  87.5 1.0 collective-permute-start.2
  88.5 0.0 collective-permute-done.refs_1_
  88.5 3.1 %collective-permute-done.1.refs_2_ = bf16[128,256]{1,0:T(8,128)(2,1)S(1)} collective-permute-done((bf16[128,256]{1,0:T(8,128)(2,1)S(1)}, bf16[128,256]{1,0:T(8,128)(2,1)S(1)}, u32[]{:S(2)}, u32[]{:S(2)}) %collective-permute-start.1) | collective-permute-done | bytes 65568 | tf_op jit(solution)/shard_map/ppermute | solution.py:317
  91.5 0.5 collective-permute-done.2.refs_3_
  92.0 0.0 copy-start.1
  92.0 2.2 %copy-done.1 = bf16[2,4,4,4,128,128]{5,4,3,2,1,0:T(8,128)(2,1)S(1)} copy-done((bf16[2,4,4,4,128,128]{5,4,3,2,1,0:T(8,128)(2,1)S(1)}, bf16[2,4,4,4,128,128]{5,4,3,2,1,0:T(8,128)(2,1)}, u32[]{:S(2)}) %copy-start.1) | copy-done | bytes 4194328
  94.2 2.2 %mix.2 = (bf16[128,256]{1,0:T(8,128)(2,1)S(1)}, bf16[128,256]{1,0:T(8,128)(2,1)S(1)}, bf16[128,256]{1,0:T(8,128)(2,1)S(1)}, bf16[128,256]{1,0:T(8,128)(2,1)S(1)}) custom-call(bf16[2,4,4,4,128,128]{5,4,3,2,1,0:T(8,128)(2,1)S(1)} %copy-done.1, bf16[128,256]{1,0:T(8,128)(2,1)S(1)} %get-tuple-element.24.refs_0_, ...), custom_call_target="tpu_custom_call" | custom-call | flops 8388608 | bytes 4194304 | tf_op jit(solution)/shard_map/mix/pallas_call | solution.py:217
  96.4 0.5 collective-permute-start.3
  96.9 0.8 collective-permute-start.4
  97.7 0.6 collective-permute-start.5
  98.4 0.0 collective-permute-done.3.refs_1_
  98.4 3.3 %collective-permute-done.4.refs_2_ = bf16[128,256]{1,0:T(8,128)(2,1)S(1)} collective-permute-done((bf16[128,256]{1,0:T(8,128)(2,1)S(1)}, bf16[128,256]{1,0:T(8,128)(2,1)S(1)}, u32[]{:S(2)}, u32[]{:S(2)}) %collective-permute-start.4) | collective-permute-done | bytes 65568 | tf_op jit(solution)/shard_map/ppermute | solution.py:317
  101.6 0.5 collective-permute-done.5.refs_3_
  102.1 1.7 %inverse_x.2 = bf16[8,256,256]{2,1,0:T(8,128)(2,1)} custom-call(s32[1]{0:T(128)} %bitcast.me_ref, bf16[256,128]{1,0:T(8,128)(2,1)S(1)} %copy-done.7, bf16[128,256]{1,0:T(8,128)(2,1)S(1)} %get-tuple-element.28.refs_0_, bf16[128,256]{1,0:T(8,128)(2,1)S(1)} %collective-permute-done.3.refs_1_, bf16[128,256]{1,0:T(8,128)(2,1)S(1)} %collective-permute-done.4.refs_2_, ...), custom_call_target="tpu_custom_call" | custom-call | flops 134217728 | bytes 2097152 | tf_op jit(solution)/shard_map/inverse_x/pallas_call | solution.py:254
  103.8 8.0 %all-to-all-done.3.back_ref = bf16[8,256,256]{2,1,0:T(8,128)(2,1)S(1)} async-done(((bf16[8,256,256]{2,1,0:T(8,128)(2,1)}), bf16[8,256,256]{2,1,0:T(8,128)(2,1)S(1)}, u32[]{:S(2)}, u32[]{:S(2)}) %all-to-all-start.3) | async-done | bytes 1048608 | tf_op jit(solution)/shard_map/all_to_all | solution.py:311
  111.8 3.7 %all-to-all-start.2 = ((bf16[8,256,256]{2,1,0:T(8,128)(2,1)}), bf16[8,256,256]{2,1,0:T(8,128)(2,1)S(1)}, u32[]{:S(2)}, u32[]{:S(2)}) async-start(bf16[8,256,256]{2,1,0:T(8,128)(2,1)} %inverse_x.2), calls=%async_computation.2 | async-start | bytes 2097152 | tf_op jit(solution)/shard_map/all_to_all | solution.py:311
  115.6 0.0 copy-done.8
  115.6 0.0 copy-done.2
  115.6 12.0 %inverse_yz.2.refs_0_ = bf16[2,4,32,256,256]{4,3,2,1,0:T(8,128)(2,1)} custom-call(bf16[8,256,256]{2,1,0:T(8,128)(2,1)S(1)} %all-to-all-done.3.back_ref, f32[4]{0:T(128)S(1)} %convert_element_type.3.shift_ref, bf16[256,128]{1,0:T(8,128)(2,1)S(1)} %copy-done.7, bf16[4,256,256]{2,1,0:T(8,128)(2,1)S(1)} %copy-done.2), custom_call_target="tpu_custom_call" | custom-call | flops 4831838208 | bytes 16777216 | tf_op jit(solution)/shard_map/inverse_yz/pallas_call | solution.py:291
  127.6 13.8 %all-to-all-done.2.back_ref = bf16[8,256,256]{2,1,0:T(8,128)(2,1)S(1)} async-done(((bf16[8,256,256]{2,1,0:T(8,128)(2,1)}), bf16[8,256,256]{2,1,0:T(8,128)(2,1)S(1)}, u32[]{:S(2)}, u32[]{:S(2)}) %all-to-all-start.2) | async-done | bytes 1048608 | tf_op jit(solution)/shard_map/all_to_all | solution.py:311
  141.4 12.0 %inverse_yz.3 = bf16[2,4,32,256,256]{4,3,2,1,0:T(8,128)(2,1)} custom-call(bf16[8,256,256]{2,1,0:T(8,128)(2,1)S(1)} %all-to-all-done.2.back_ref, f32[4]{0:T(128)S(1)} %convert_element_type.3.shift_ref, bf16[256,128]{1,0:T(8,128)(2,1)S(1)} %copy-done.7, bf16[4,256,256]{2,1,0:T(8,128)(2,1)S(1)} %copy-done.2, ...), custom_call_target="tpu_custom_call", output_to_operand_aliasing={{}: (4, {})} | custom-call | flops 4831838208 | bytes 16777216 | tf_op jit(solution)/shard_map/inverse_yz/pallas_call | solution.py:291
  (1 shorter events, 0.0 us)
Async XLA Ops:
  0.0 1.0 copy-start.3
  1.0 0.8 copy-start.5
  1.9 17.1 %copy-start.4 = (bf16[1024,256]{1,0:T(8,128)(2,1)S(1)}, bf16[1024,256]{1,0:T(8,128)(2,1)}, u32[]{:S(2)}) copy-start(bf16[1024,256]{1,0:T(8,128)(2,1)} %constant.12.clone.fwd_z_ref) | copy-start | bytes 1572868
  1.9 17.1 %copy-start.6 = (bf16[128,256]{1,0:T(8,128)(2,1)S(1)}, bf16[128,256]{1,0:T(8,128)(2,1)}, u32[]{:S(2)}) copy-start(bf16[128,256]{1,0:T(8,128)(2,1)} %constant.13.clone.fwd_two_ref.table_ref) | copy-start | bytes 196612
  11.6 66.7 %copy-start.7 = (bf16[256,128]{1,0:T(8,128)(2,1)S(1)}, bf16[256,128]{1,0:T(8,128)(2,1)}, u32[]{:S(2)}) copy-start(bf16[256,128]{1,0:T(8,128)(2,1)} %constant.14.clone.table_ref.inv_two_ref) | copy-start | bytes 196612
  11.6 33.2 %all-to-all-start = ((bf16[8,256,256]{2,1,0:T(8,128)(2,1)}), bf16[8,256,256]{2,1,0:T(8,128)(2,1)S(1)}, u32[]{:S(2)}, u32[]{:S(2)}) async-start(bf16[8,256,256]{2,1,0:T(8,128)(2,1)} %forward_zy.2), calls=%async_computation | async-start | bytes 2097152 | tf_op jit(solution)/shard_map/all_to_all | solution.py:311
  19.0 96.6 %copy-start.8 = (bf16[4]{0:T(256)(128)(2,1)S(1)}, bf16[4]{0:T(256)(128)(2,1)}, u32[]{:S(2)}) copy-start(bf16[4]{0:T(256)(128)(2,1)} %param.9) | copy-start | bytes 28
  19.0 96.6 %copy-start.2 = (bf16[4,256,256]{2,1,0:T(8,128)(2,1)S(1)}, bf16[4,256,256]{2,1,0:T(8,128)(2,1)}, u32[]{:S(2)}) copy-start(bf16[4,256,256]{2,1,0:T(8,128)(2,1)} %constant.15.clone.inv_z_ref) | copy-start | bytes 1572868
  44.8 35.1 %all-to-all-start.1 = ((bf16[8,256,256]{2,1,0:T(8,128)(2,1)}), bf16[8,256,256]{2,1,0:T(8,128)(2,1)S(1)}, u32[]{:S(2)}, u32[]{:S(2)}) async-start(bf16[8,256,256]{2,1,0:T(8,128)(2,1)} %forward_zy.3), calls=%async_computation.1 | async-start | bytes 2097152 | tf_op jit(solution)/shard_map/all_to_all | solution.py:311
  62.1 1.9 %collective-permute-start.6 = (bf16[128,256]{1,0:T(8,128)(2,1)S(1)}, bf16[128,256]{1,0:T(8,128)(2,1)S(1)}, u32[]{:S(2)}, u32[]{:S(2)}) collective-permute-start(bf16[128,256]{1,0:T(8,128)(2,1)S(1)} %get-tuple-element.34), channel_id=1, source_target_pairs={{0,1},{1,0},{2,3},{3,2},{4,5},{5,4},{6,7},{7,6},{8,9},{9,8},{10,11... | collective-permute-start | bytes 196616 | tf_op jit(solution)/shard_map/ppermute | solution.py:317
  62.2 4.5 %collective-permute-start.7 = (bf16[128,256]{1,0:T(8,128)(2,1)S(1)}, bf16[128,256]{1,0:T(8,128)(2,1)S(1)}, u32[]{:S(2)}, u32[]{:S(2)}) collective-permute-start(bf16[128,256]{1,0:T(8,128)(2,1)S(1)} %get-tuple-element.35), channel_id=1, source_target_pairs={{0,2},{1,3},{2,0},{3,1},{4,6},{5,7},{6,4},{7,5},{8,10},{9,11},{10,... | collective-permute-start | bytes 196616 | tf_op jit(solution)/shard_map/ppermute | solution.py:317
  63.8 4.0 %collective-permute-start.8 = (bf16[128,256]{1,0:T(8,128)(2,1)S(1)}, bf16[128,256]{1,0:T(8,128)(2,1)S(1)}, u32[]{:S(2)}, u32[]{:S(2)}) collective-permute-start(bf16[128,256]{1,0:T(8,128)(2,1)S(1)} %get-tuple-element.36), channel_id=1, source_target_pairs={{0,3},{1,2},{2,1},{3,0},{4,7},{5,6},{6,5},{7,4},{8,11},{9,10},{10,... | collective-permute-start | bytes 196616 | tf_op jit(solution)/shard_map/ppermute | solution.py:317
  70.0 2.0 %copy-start = (bf16[2,4,4,4,128,128]{5,4,3,2,1,0:T(8,128)(2,1)}, bf16[2,4,4,4,128,128]{5,4,3,2,1,0:T(8,128)(2,1)S(1)}, u32[]{:S(2)}) copy-start(bf16[2,4,4,4,128,128]{5,4,3,2,1,0:T(8,128)(2,1)S(1)} %place_weights.1.w_ref) | copy-start | bytes 12582916
  72.0 1.9 %collective-permute-start.9 = (bf16[128,256]{1,0:T(8,128)(2,1)S(1)}, bf16[128,256]{1,0:T(8,128)(2,1)S(1)}, u32[]{:S(2)}, u32[]{:S(2)}) collective-permute-start(bf16[128,256]{1,0:T(8,128)(2,1)S(1)} %get-tuple-element.38), channel_id=1, source_target_pairs={{0,1},{1,0},{2,3},{3,2},{4,5},{5,4},{6,7},{7,6},{8,9},{9,8},{10,11... | collective-permute-start | bytes 196616 | tf_op jit(solution)/shard_map/ppermute | solution.py:317
  72.5 4.3 %collective-permute-start.10 = (bf16[128,256]{1,0:T(8,128)(2,1)S(1)}, bf16[128,256]{1,0:T(8,128)(2,1)S(1)}, u32[]{:S(2)}, u32[]{:S(2)}) collective-permute-start(bf16[128,256]{1,0:T(8,128)(2,1)S(1)} %get-tuple-element.39), channel_id=1, source_target_pairs={{0,2},{1,3},{2,0},{3,1},{4,6},{5,7},{6,4},{7,5},{8,10},{9,11},{10,... | collective-permute-start | bytes 196616 | tf_op jit(solution)/shard_map/ppermute | solution.py:317
  73.9 4.3 %collective-permute-start.11 = (bf16[128,256]{1,0:T(8,128)(2,1)S(1)}, bf16[128,256]{1,0:T(8,128)(2,1)S(1)}, u32[]{:S(2)}, u32[]{:S(2)}) collective-permute-start(bf16[128,256]{1,0:T(8,128)(2,1)S(1)} %get-tuple-element.40), channel_id=1, source_target_pairs={{0,3},{1,2},{2,1},{3,0},{4,7},{5,6},{6,5},{7,4},{8,11},{9,10},{10,... | collective-permute-start | bytes 196616 | tf_op jit(solution)/shard_map/ppermute | solution.py:317
  79.9 31.9 %all-to-all-start.3 = ((bf16[8,256,256]{2,1,0:T(8,128)(2,1)}), bf16[8,256,256]{2,1,0:T(8,128)(2,1)S(1)}, u32[]{:S(2)}, u32[]{:S(2)}) async-start(bf16[8,256,256]{2,1,0:T(8,128)(2,1)} %inverse_x.3), calls=%async_computation.3 | async-start | bytes 2097152 | tf_op jit(solution)/shard_map/all_to_all | solution.py:311
  86.5 1.9 %collective-permute-start = (bf16[128,256]{1,0:T(8,128)(2,1)S(1)}, bf16[128,256]{1,0:T(8,128)(2,1)S(1)}, u32[]{:S(2)}, u32[]{:S(2)}) collective-permute-start(bf16[128,256]{1,0:T(8,128)(2,1)S(1)} %get-tuple-element.25), channel_id=1, source_target_pairs={{0,1},{1,0},{2,3},{3,2},{4,5},{5,4},{6,7},{7,6},{8,9},{9,8},{10,11... | collective-permute-start | bytes 196616 | tf_op jit(solution)/shard_map/ppermute | solution.py:317
  86.6 5.0 %collective-permute-start.1 = (bf16[128,256]{1,0:T(8,128)(2,1)S(1)}, bf16[128,256]{1,0:T(8,128)(2,1)S(1)}, u32[]{:S(2)}, u32[]{:S(2)}) collective-permute-start(bf16[128,256]{1,0:T(8,128)(2,1)S(1)} %get-tuple-element.26), channel_id=1, source_target_pairs={{0,2},{1,3},{2,0},{3,1},{4,6},{5,7},{6,4},{7,5},{8,10},{9,11},{10,... | collective-permute-start | bytes 196616 | tf_op jit(solution)/shard_map/ppermute | solution.py:317
  87.5 4.6 %collective-permute-start.2 = (bf16[128,256]{1,0:T(8,128)(2,1)S(1)}, bf16[128,256]{1,0:T(8,128)(2,1)S(1)}, u32[]{:S(2)}, u32[]{:S(2)}) collective-permute-start(bf16[128,256]{1,0:T(8,128)(2,1)S(1)} %get-tuple-element.27), channel_id=1, source_target_pairs={{0,3},{1,2},{2,1},{3,0},{4,7},{5,6},{6,5},{7,4},{8,11},{9,10},{10,... | collective-permute-start | bytes 196616 | tf_op jit(solution)/shard_map/ppermute | solution.py:317
  92.0 2.2 %copy-start.1 = (bf16[2,4,4,4,128,128]{5,4,3,2,1,0:T(8,128)(2,1)S(1)}, bf16[2,4,4,4,128,128]{5,4,3,2,1,0:T(8,128)(2,1)}, u32[]{:S(2)}) copy-start(bf16[2,4,4,4,128,128]{5,4,3,2,1,0:T(8,128)(2,1)} %copy-done) | copy-start | bytes 12582916
  96.4 1.9 %collective-permute-start.3 = (bf16[128,256]{1,0:T(8,128)(2,1)S(1)}, bf16[128,256]{1,0:T(8,128)(2,1)S(1)}, u32[]{:S(2)}, u32[]{:S(2)}) collective-permute-start(bf16[128,256]{1,0:T(8,128)(2,1)S(1)} %get-tuple-element.29), channel_id=1, source_target_pairs={{0,1},{1,0},{2,3},{3,2},{4,5},{5,4},{6,7},{7,6},{8,9},{9,8},{10,11... | collective-permute-start | bytes 196616 | tf_op jit(solution)/shard_map/ppermute | solution.py:317
  96.9 4.7 %collective-permute-start.4 = (bf16[128,256]{1,0:T(8,128)(2,1)S(1)}, bf16[128,256]{1,0:T(8,128)(2,1)S(1)}, u32[]{:S(2)}, u32[]{:S(2)}) collective-permute-start(bf16[128,256]{1,0:T(8,128)(2,1)S(1)} %get-tuple-element.30), channel_id=1, source_target_pairs={{0,2},{1,3},{2,0},{3,1},{4,6},{5,7},{6,4},{7,5},{8,10},{9,11},{10,... | collective-permute-start | bytes 196616 | tf_op jit(solution)/shard_map/ppermute | solution.py:317
  97.7 4.4 %collective-permute-start.5 = (bf16[128,256]{1,0:T(8,128)(2,1)S(1)}, bf16[128,256]{1,0:T(8,128)(2,1)S(1)}, u32[]{:S(2)}, u32[]{:S(2)}) collective-permute-start(bf16[128,256]{1,0:T(8,128)(2,1)S(1)} %get-tuple-element.31), channel_id=1, source_target_pairs={{0,3},{1,2},{2,1},{3,0},{4,7},{5,6},{6,5},{7,4},{8,11},{9,10},{10,... | collective-permute-start | bytes 196616 | tf_op jit(solution)/shard_map/ppermute | solution.py:317
  111.8 29.6 %all-to-all-start.2 = ((bf16[8,256,256]{2,1,0:T(8,128)(2,1)}), bf16[8,256,256]{2,1,0:T(8,128)(2,1)S(1)}, u32[]{:S(2)}, u32[]{:S(2)}) async-start(bf16[8,256,256]{2,1,0:T(8,128)(2,1)} %inverse_x.2), calls=%async_computation.2 | async-start | bytes 2097152 | tf_op jit(solution)/shard_map/all_to_all | solution.py:311

commit v3 on v2

--- a/solution.py
+++ b/solution.py
@@ -157,29 +157,30 @@
     lanes = chans * kept
 
     def kernel(me_ref, w_ref, out_ref):
-        for q in range(2):
-            tiles = {}
-            for i in range(chans):
-                for o in range(chans):
-                    tiles[i, o] = w_ref[i, o, :, q].astype(F32).reshape(rows, kept)
-            for r in range(chans):
-                row = jnp.concatenate([tiles[(o + r) % chans, o] for o in range(chans)], axis=1)
-                out_ref[q, 0, 0, r] = row.astype(BF16)
+        for g in range(groups):
+            first = (me_ref[0] ^ g) * chans
+            for q in range(2):
+                for r in range(chans):
+                    tiles = [
+                        w_ref[(o + r) % chans, first + o, :, q].astype(F32).reshape(rows, kept)
+                        for o in range(chans)
+                    ]
+                    out_ref[q, 0, g, r] = jnp.concatenate(tiles, axis=1).astype(BF16)
 
     return call(
         kernel,
         (2 * weights.size, 10 * weights.size),
         grid_spec=pltpu.PrefetchScalarGridSpec(
             num_scalar_prefetch=1,
-            grid=(groups, outputs // chans),
+            grid=(groups,),
             in_specs=[
                 pl.BlockSpec(
-                    (chans, chans, modes, 2, own, kept),
-                    lambda i, o, me_ref: (me_ref[0] ^ i, me_ref[0] ^ o, 0, 0, 0, 0),
+                    (chans, outputs, modes, 2, own, kept),
+                    lambda i, me_ref: (me_ref[0] ^ i, 0, 0, 0, 0, 0),
                 )
             ],
             out_specs=pl.BlockSpec(
-                (2, 1, 1, chans, rows, lanes), lambda i, o, me_ref: (0, i, o, 0, 0, 0)
+                (2, 1, groups, chans, rows, lanes), lambda i, me_ref: (0, i, 0, 0, 0, 0)
             ),
         ),
         out_shape=jax.ShapeDtypeStruct(
@@ -324,11 +325,12 @@
     shift = shift.astype(F32)
     me = lax.axis_index("chan").reshape(1)
     placed = place_weights(jnp.transpose(weights, (0, 1, 2, 4, 5, 3)), me, chans)
-    coef_y = [
-        exchange(forward_zy(state, b, slabs, fwd_z, fwd_two), "slab") for b in range(samples)
-    ]
-    coef_y[0], placed = lax.optimization_barrier((coef_y[0], placed))
-    back_x = []
+    coef_y, back_x = [], []
+    for b in range(samples):
+        sent = forward_zy(state, b, slabs, fwd_z, fwd_two)
+        if b == 1:
+            sent, placed = lax.optimization_barrier((sent, placed))
+        coef_y.append(exchange(sent, "slab"))
     for b in range(samples):
         spectra = swap(forward_x(coef_y[b], me, groups, fwd_two), "chan")
         mixed = swap(mix(spectra, placed, KM), "chan")

time: 154 us -> 146 us (0.948)
  Pallas kernels: 65.5 us -> 60.1 us
  waiting for transfers between devices: 53.3 us -> 50.9 us
  starting transfers between devices: 28.4 us -> 26.1 us
  local copies, waits for them, and re-layouts: 6.1 us -> 8.29 us
    pallas_call x1, Pallas kernels: 13.1 us -> 7.87 us  [place_weights(): call(kernel, (2 * weights.size, 10 * weights.size), grid_spec=pltpu.Prefe...]
    all_to_all x4, waiting for transfers between devices: 37.9 us -> 34.8 us  [exchange(): return lax.all_to_all(blocks, axis, split_axis=0, concat_axis=0, tiled=True)]
    all_to_all x4, starting transfers between devices: 20.7 us -> 18.4 us  [exchange(): return lax.all_to_all(blocks, axis, split_axis=0, concat_axis=0, tiled=True)]
    unnamed x18 -> x20, local copies, waits for them, and re-layouts: 6.1 us -> 8.29 us
  transfers between devices with their start and end apart: 16 -> 16, of which waited for: 11 -> 12; matrix products, arithmetic and copies ran while one was open for 0% -> 0% of each run, Pallas kernels for 29% -> 26%
where the time goes in v3:
time: 146 us; the launch traced here: 145 us
  Pallas kernels  60.1 us (41%)
  waiting for transfers between devices  50.9 us (35%)
  starting transfers between devices  26.1 us (18%)
  local copies, waits for them, and re-layouts  8.29 us (6%)
    all_to_all x4, waiting for transfers between devices, exchange(): return lax.all_to_all(blocks, axis, split_axis=0, concat_axis=0, tiled=True)  34.8 us
    pallas_call x2, Pallas kernels, inverse_yz(): call(kernel, (2 * planes * NG * (2 * two * lanes + chans * lanes * NG), 2...  23.9 us
    pallas_call x2, Pallas kernels, forward_zy(): call(kernel, (2 * planes * NG * lanes * (chans * NG + 2 * two), 2 * chans...  19.3 us
    all_to_all x4, starting transfers between devices, exchange(): return lax.all_to_all(blocks, axis, split_axis=0, concat_axis=0, tiled=True)  18.4 us
    ppermute x12, waiting for transfers between devices, swap(): lax.ppermute(blocks[r], axis, [(i, i ^ r) for i in range(count)])  16.1 us
    unnamed x20, local copies, waits for them, and re-layouts  8.29 us
    pallas_call x1, Pallas kernels, place_weights(): call(kernel, (2 * weights.size, 10 * weights.size), grid_spec=pltpu.Prefe...  7.87 us
    ppermute x12, starting transfers between devices, swap(): lax.ppermute(blocks[r], axis, [(i, i ^ r) for i in range(count)])  7.72 us
  transfers between devices with their start and end apart: 16, of which 12 were waited for; matrix products, arithmetic and copies ran while one was open for 0% of the time, Pallas kernels for 26%

profile of v3, /device:TPU:0, one launch (start us, length us, event | category | flops | bytes accessed | tf_op | source)
XLA Modules:
  0.0 145.4 jit_solution(18160865944985874088)
XLA Ops:
  0.0 0.0 copy-start.4
  0.0 1.0 copy-done.4
  1.0 0.0 copy-start.6
  1.0 0.8 copy-done.6
  1.9 0.0 copy-start.5
  1.9 0.0 copy-start.7
  1.9 9.7 %forward_zy.3 = bf16[8,256,256]{2,1,0:T(8,128)(2,1)} custom-call(bf16[2,4,32,256,256]{4,3,2,1,0:T(8,128)(2,1)} %state_ref.3, bf16[1024,256]{1,0:T(8,128)(2,1)S(1)} %copy-done.4, bf16[128,256]{1,0:T(8,128)(2,1)S(1)} %copy-done.6), custom_call_target="tpu_custom_call" | custom-call | flops 4831838208 | bytes 16777216 | tf_op jit(solution)/shard_map/forward_zy/pallas_call | solution.py:97
  11.6 0.0 copy-start.8
  11.6 7.4 %all-to-all-start.2 = ((bf16[8,256,256]{2,1,0:T(8,128)(2,1)}), bf16[8,256,256]{2,1,0:T(8,128)(2,1)S(1)}, u32[]{:S(2)}, u32[]{:S(2)}) async-start(bf16[8,256,256]{2,1,0:T(8,128)(2,1)} %forward_zy.3), calls=%async_computation.2 | async-start | bytes 2097152 | tf_op jit(solution)/shard_map/all_to_all | solution.py:312
  19.0 0.0 copy-start.9
  19.0 0.0 copy-start.3
  19.0 7.9 %place_weights.1.w_ref = bf16[2,4,4,4,128,128]{5,4,3,2,1,0:T(8,128)(2,1)S(1)} custom-call(s32[1]{0:T(128)} %bitcast.me_ref, bf16[16,16,16,2,8,32]{5,4,3,2,1,0:T(8,128)(2,1)} %bitcast.2), custom_call_target="tpu_custom_call" | custom-call | flops 4194304 | bytes 20971520 | tf_op jit(solution)/shard_map/place_weights/pallas_call | solution.py:170
  26.9 0.0 copy-start
  26.9 2.0 %copy-done = bf16[2,4,4,4,128,128]{5,4,3,2,1,0:T(8,128)(2,1)} copy-done((bf16[2,4,4,4,128,128]{5,4,3,2,1,0:T(8,128)(2,1)}, bf16[2,4,4,4,128,128]{5,4,3,2,1,0:T(8,128)(2,1)S(1)}, u32[]{:S(2)}) %copy-start) | copy-done | bytes 4194328
  28.9 0.0 copy-done.5
  28.9 0.0 copy-done.7
  28.9 9.6 %forward_zy.2 = bf16[8,256,256]{2,1,0:T(8,128)(2,1)} custom-call(bf16[2,4,32,256,256]{4,3,2,1,0:T(8,128)(2,1)} %state_ref.3, bf16[1024,256]{1,0:T(8,128)(2,1)S(1)} %copy-done.5, bf16[128,256]{1,0:T(8,128)(2,1)S(1)} %copy-done.7), custom_call_target="tpu_custom_call" | custom-call | flops 4831838208 | bytes 16777216 | tf_op jit(solution)/shard_map/forward_zy/pallas_call | solution.py:97
  38.5 6.2 %all-to-all-done.2.coef_ref = bf16[8,256,256]{2,1,0:T(8,128)(2,1)S(1)} async-done(((bf16[8,256,256]{2,1,0:T(8,128)(2,1)}), bf16[8,256,256]{2,1,0:T(8,128)(2,1)S(1)}, u32[]{:S(2)}, u32[]{:S(2)}) %all-to-all-start.2) | async-done | bytes 1048608 | tf_op jit(solution)/shard_map/all_to_all | solution.py:312
  44.8 3.6 %all-to-all-start = ((bf16[8,256,256]{2,1,0:T(8,128)(2,1)}), bf16[8,256,256]{2,1,0:T(8,128)(2,1)S(1)}, u32[]{:S(2)}, u32[]{:S(2)}) async-start(bf16[8,256,256]{2,1,0:T(8,128)(2,1)} %forward_zy.2), calls=%async_computation | async-start | bytes 2097152 | tf_op jit(solution)/shard_map/all_to_all | solution.py:312
  48.4 0.6 forward_x.3
  49.0 0.1 collective-permute-start.6
  49.1 1.6 %collective-permute-start.7 = (bf16[128,256]{1,0:T(8,128)(2,1)S(1)}, bf16[128,256]{1,0:T(8,128)(2,1)S(1)}, u32[]{:S(2)}, u32[]{:S(2)}) collective-permute-start(bf16[128,256]{1,0:T(8,128)(2,1)S(1)} %get-tuple-element.35), channel_id=1, source_target_pairs={{0,2},{1,3},{2,0},{3,1},{4,6},{5,7},{6,4},{7,5},{8,10},{9,11},{10,... | collective-permute-start | bytes 196616 | tf_op jit(solution)/shard_map/ppermute | solution.py:318
  50.6 0.3 collective-permute-start.8
  50.9 0.0 collective-permute-done.6.refs_1_
  50.9 2.6 %collective-permute-done.7.refs_2_ = bf16[128,256]{1,0:T(8,128)(2,1)S(1)} collective-permute-done((bf16[128,256]{1,0:T(8,128)(2,1)S(1)}, bf16[128,256]{1,0:T(8,128)(2,1)S(1)}, u32[]{:S(2)}, u32[]{:S(2)}) %collective-permute-start.7) | collective-permute-done | bytes 65568 | tf_op jit(solution)/shard_map/ppermute | solution.py:318
  53.6 1.1 collective-permute-done.8.refs_3_
  54.7 0.0 copy-start.1
  54.7 2.2 %copy-done.1 = bf16[2,4,4,4,128,128]{5,4,3,2,1,0:T(8,128)(2,1)S(1)} copy-done((bf16[2,4,4,4,128,128]{5,4,3,2,1,0:T(8,128)(2,1)S(1)}, bf16[2,4,4,4,128,128]{5,4,3,2,1,0:T(8,128)(2,1)}, u32[]{:S(2)}) %copy-start.1) | copy-done | bytes 4194328
  56.9 2.2 %mix.3 = (bf16[128,256]{1,0:T(8,128)(2,1)S(1)}, bf16[128,256]{1,0:T(8,128)(2,1)S(1)}, bf16[128,256]{1,0:T(8,128)(2,1)S(1)}, bf16[128,256]{1,0:T(8,128)(2,1)S(1)}) custom-call(bf16[2,4,4,4,128,128]{5,4,3,2,1,0:T(8,128)(2,1)S(1)} %copy-done.1, bf16[128,256]{1,0:T(8,128)(2,1)S(1)} %get-tuple-element.33.refs_0_, ...), custom_call_target="tpu_custom_call" | custom-call | flops 8388608 | bytes 4194304 | tf_op jit(solution)/shard_map/mix/pallas_call | solution.py:218
  59.0 0.3 collective-permute-start.9
  59.4 1.5 %collective-permute-start.10 = (bf16[128,256]{1,0:T(8,128)(2,1)S(1)}, bf16[128,256]{1,0:T(8,128)(2,1)S(1)}, u32[]{:S(2)}, u32[]{:S(2)}) collective-permute-start(bf16[128,256]{1,0:T(8,128)(2,1)S(1)} %get-tuple-element.39), channel_id=1, source_target_pairs={{0,2},{1,3},{2,0},{3,1},{4,6},{5,7},{6,4},{7,5},{8,10},{9,11},{10,... | collective-permute-start | bytes 196616 | tf_op jit(solution)/shard_map/ppermute | solution.py:318
  60.9 0.1 collective-permute-start.11
  61.0 0.0 collective-permute-done.9.refs_1_
  61.0 2.7 %collective-permute-done.10.refs_2_ = bf16[128,256]{1,0:T(8,128)(2,1)S(1)} collective-permute-done((bf16[128,256]{1,0:T(8,128)(2,1)S(1)}, bf16[128,256]{1,0:T(8,128)(2,1)S(1)}, u32[]{:S(2)}, u32[]{:S(2)}) %collective-permute-start.10) | collective-permute-done | bytes 65568 | tf_op jit(solution)/shard_map/ppermute | solution.py:318
  63.7 1.6 %collective-permute-done.11.refs_3_ = bf16[128,256]{1,0:T(8,128)(2,1)S(1)} collective-permute-done((bf16[128,256]{1,0:T(8,128)(2,1)S(1)}, bf16[128,256]{1,0:T(8,128)(2,1)S(1)}, u32[]{:S(2)}, u32[]{:S(2)}) %collective-permute-start.11) | collective-permute-done | bytes 65568 | tf_op jit(solution)/shard_map/ppermute | solution.py:318
  65.3 0.0 copy-done.8
  65.3 1.7 %inverse_x.3 = bf16[8,256,256]{2,1,0:T(8,128)(2,1)} custom-call(s32[1]{0:T(128)} %bitcast.me_ref, bf16[256,128]{1,0:T(8,128)(2,1)S(1)} %copy-done.8, bf16[128,256]{1,0:T(8,128)(2,1)S(1)} %get-tuple-element.37.refs_0_, bf16[128,256]{1,0:T(8,128)(2,1)S(1)} %collective-permute-done.9.refs_1_, bf16[128,256]{1,0:T(8,128)(2,1)S(1)} %collective-permute-done.10.refs_2_, ...), custom_call_target="tpu_custom_call" | custom-call | flops 134217728 | bytes 2097152 | tf_op jit(solution)/shard_map/inverse_x/pallas_call | solution.py:255
  66.9 7.4 %all-to-all-done.coef_ref = bf16[8,256,256]{2,1,0:T(8,128)(2,1)S(1)} async-done(((bf16[8,256,256]{2,1,0:T(8,128)(2,1)}), bf16[8,256,256]{2,1,0:T(8,128)(2,1)S(1)}, u32[]{:S(2)}, u32[]{:S(2)}) %all-to-all-start) | async-done | bytes 1048608 | tf_op jit(solution)/shard_map/all_to_all | solution.py:312
  74.3 3.6 %all-to-all-start.3 = ((bf16[8,256,256]{2,1,0:T(8,128)(2,1)}), bf16[8,256,256]{2,1,0:T(8,128)(2,1)S(1)}, u32[]{:S(2)}, u32[]{:S(2)}) async-start(bf16[8,256,256]{2,1,0:T(8,128)(2,1)} %inverse_x.3), calls=%async_computation.3 | async-start | bytes 2097152 | tf_op jit(solution)/shard_map/all_to_all | solution.py:312
  77.9 0.6 forward_x.2
  78.6 0.1 collective-permute-start
  78.6 1.6 %collective-permute-start.1 = (bf16[128,256]{1,0:T(8,128)(2,1)S(1)}, bf16[128,256]{1,0:T(8,128)(2,1)S(1)}, u32[]{:S(2)}, u32[]{:S(2)}) collective-permute-start(bf16[128,256]{1,0:T(8,128)(2,1)S(1)} %get-tuple-element.27), channel_id=1, source_target_pairs={{0,2},{1,3},{2,0},{3,1},{4,6},{5,7},{6,4},{7,5},{8,10},{9,11},{10,... | collective-permute-start | bytes 196616 | tf_op jit(solution)/shard_map/ppermute | solution.py:318
  80.2 0.3 collective-permute-start.2
  80.5 0.0 collective-permute-done.refs_1_
  80.5 2.6 %collective-permute-done.1.refs_2_ = bf16[128,256]{1,0:T(8,128)(2,1)S(1)} collective-permute-done((bf16[128,256]{1,0:T(8,128)(2,1)S(1)}, bf16[128,256]{1,0:T(8,128)(2,1)S(1)}, u32[]{:S(2)}, u32[]{:S(2)}) %collective-permute-start.1) | collective-permute-done | bytes 65568 | tf_op jit(solution)/shard_map/ppermute | solution.py:318
  83.2 1.1 collective-permute-done.2.refs_3_
  84.3 0.0 copy-start.2
  84.3 2.2 %copy-done.2 = bf16[2,4,4,4,128,128]{5,4,3,2,1,0:T(8,128)(2,1)S(1)} copy-done((bf16[2,4,4,4,128,128]{5,4,3,2,1,0:T(8,128)(2,1)S(1)}, bf16[2,4,4,4,128,128]{5,4,3,2,1,0:T(8,128)(2,1)}, u32[]{:S(2)}) %copy-start.2) | copy-done | bytes 4194328
  86.4 2.2 %mix.2 = (bf16[128,256]{1,0:T(8,128)(2,1)S(1)}, bf16[128,256]{1,0:T(8,128)(2,1)S(1)}, bf16[128,256]{1,0:T(8,128)(2,1)S(1)}, bf16[128,256]{1,0:T(8,128)(2,1)S(1)}) custom-call(bf16[2,4,4,4,128,128]{5,4,3,2,1,0:T(8,128)(2,1)S(1)} %copy-done.2, bf16[128,256]{1,0:T(8,128)(2,1)S(1)} %get-tuple-element.25.refs_0_, ...), custom_call_target="tpu_custom_call" | custom-call | flops 8388608 | bytes 4194304 | tf_op jit(solution)/shard_map/mix/pallas_call | solution.py:218
  88.6 0.3 collective-permute-start.3
  89.0 1.5 %collective-permute-start.4 = (bf16[128,256]{1,0:T(8,128)(2,1)S(1)}, bf16[128,256]{1,0:T(8,128)(2,1)S(1)}, u32[]{:S(2)}, u32[]{:S(2)}) collective-permute-start(bf16[128,256]{1,0:T(8,128)(2,1)S(1)} %get-tuple-element.31), channel_id=1, source_target_pairs={{0,2},{1,3},{2,0},{3,1},{4,6},{5,7},{6,4},{7,5},{8,10},{9,11},{10,... | collective-permute-start | bytes 196616 | tf_op jit(solution)/shard_map/ppermute | solution.py:318
  90.5 0.1 collective-permute-start.5
  90.6 0.0 collective-permute-done.3.refs_1_
  90.6 2.7 %collective-permute-done.4.refs_2_ = bf16[128,256]{1,0:T(8,128)(2,1)S(1)} collective-permute-done((bf16[128,256]{1,0:T(8,128)(2,1)S(1)}, bf16[128,256]{1,0:T(8,128)(2,1)S(1)}, u32[]{:S(2)}, u32[]{:S(2)}) %collective-permute-start.4) | collective-permute-done | bytes 65568 | tf_op jit(solution)/shard_map/ppermute | solution.py:318
  93.2 1.6 %collective-permute-done.5.refs_3_ = bf16[128,256]{1,0:T(8,128)(2,1)S(1)} collective-permute-done((bf16[128,256]{1,0:T(8,128)(2,1)S(1)}, bf16[128,256]{1,0:T(8,128)(2,1)S(1)}, u32[]{:S(2)}, u32[]{:S(2)}) %collective-permute-start.5) | collective-permute-done | bytes 65568 | tf_op jit(solution)/shard_map/ppermute | solution.py:318
  94.9 1.7 %inverse_x.2 = bf16[8,256,256]{2,1,0:T(8,128)(2,1)} custom-call(s32[1]{0:T(128)} %bitcast.me_ref, bf16[256,128]{1,0:T(8,128)(2,1)S(1)} %copy-done.8, bf16[128,256]{1,0:T(8,128)(2,1)S(1)} %get-tuple-element.29.refs_0_, bf16[128,256]{1,0:T(8,128)(2,1)S(1)} %collective-permute-done.3.refs_1_, bf16[128,256]{1,0:T(8,128)(2,1)S(1)} %collective-permute-done.4.refs_2_, ...), custom_call_target="tpu_custom_call" | custom-call | flops 134217728 | bytes 2097152 | tf_op jit(solution)/shard_map/inverse_x/pallas_call | solution.py:255
  96.5 7.4 %all-to-all-done.3.back_ref = bf16[8,256,256]{2,1,0:T(8,128)(2,1)S(1)} async-done(((bf16[8,256,256]{2,1,0:T(8,128)(2,1)}), bf16[8,256,256]{2,1,0:T(8,128)(2,1)S(1)}, u32[]{:S(2)}, u32[]{:S(2)}) %all-to-all-start.3) | async-done | bytes 1048608 | tf_op jit(solution)/shard_map/all_to_all | solution.py:312
  103.9 3.7 %all-to-all-start.1 = ((bf16[8,256,256]{2,1,0:T(8,128)(2,1)}), bf16[8,256,256]{2,1,0:T(8,128)(2,1)S(1)}, u32[]{:S(2)}, u32[]{:S(2)}) async-start(bf16[8,256,256]{2,1,0:T(8,128)(2,1)} %inverse_x.2), calls=%async_computation.1 | async-start | bytes 2097152 | tf_op jit(solution)/shard_map/all_to_all | solution.py:312
  107.6 0.0 copy-done.9
  107.7 0.0 copy-done.3
  107.7 12.0 %inverse_yz.2.refs_0_ = bf16[2,4,32,256,256]{4,3,2,1,0:T(8,128)(2,1)} custom-call(bf16[8,256,256]{2,1,0:T(8,128)(2,1)S(1)} %all-to-all-done.3.back_ref, f32[4]{0:T(128)S(1)} %convert_element_type.3.shift_ref, bf16[256,128]{1,0:T(8,128)(2,1)S(1)} %copy-done.8, bf16[4,256,256]{2,1,0:T(8,128)(2,1)S(1)} %copy-done.3), custom_call_target="tpu_custom_call" | custom-call | flops 4831838208 | bytes 16777216 | tf_op jit(solution)/shard_map/inverse_yz/pallas_call | solution.py:292
  119.6 13.8 %all-to-all-done.1.back_ref = bf16[8,256,256]{2,1,0:T(8,128)(2,1)S(1)} async-done(((bf16[8,256,256]{2,1,0:T(8,128)(2,1)}), bf16[8,256,256]{2,1,0:T(8,128)(2,1)S(1)}, u32[]{:S(2)}, u32[]{:S(2)}) %all-to-all-start.1) | async-done | bytes 1048608 | tf_op jit(solution)/shard_map/all_to_all | solution.py:312
  133.5 12.0 %inverse_yz.3 = bf16[2,4,32,256,256]{4,3,2,1,0:T(8,128)(2,1)} custom-call(bf16[8,256,256]{2,1,0:T(8,128)(2,1)S(1)} %all-to-all-done.1.back_ref, f32[4]{0:T(128)S(1)} %convert_element_type.3.shift_ref, bf16[256,128]{1,0:T(8,128)(2,1)S(1)} %copy-done.8, bf16[4,256,256]{2,1,0:T(8,128)(2,1)S(1)} %copy-done.3, ...), custom_call_target="tpu_custom_call", output_to_operand_aliasing={{}: (4, {})} | custom-call | flops 4831838208 | bytes 16777216 | tf_op jit(solution)/shard_map/inverse_yz/pallas_call | solution.py:292
  (1 shorter events, 0.0 us)
Async XLA Ops:
  0.0 1.0 copy-start.4
  1.0 0.8 copy-start.6
  1.9 27.0 %copy-start.5 = (bf16[1024,256]{1,0:T(8,128)(2,1)S(1)}, bf16[1024,256]{1,0:T(8,128)(2,1)}, u32[]{:S(2)}) copy-start(bf16[1024,256]{1,0:T(8,128)(2,1)} %constant.12.clone.fwd_z_ref) | copy-start | bytes 1572868
  1.9 27.0 %copy-start.7 = (bf16[128,256]{1,0:T(8,128)(2,1)S(1)}, bf16[128,256]{1,0:T(8,128)(2,1)}, u32[]{:S(2)}) copy-start(bf16[128,256]{1,0:T(8,128)(2,1)} %constant.13.clone.fwd_two_ref.table_ref) | copy-start | bytes 196612
  11.6 53.7 %copy-start.8 = (bf16[256,128]{1,0:T(8,128)(2,1)S(1)}, bf16[256,128]{1,0:T(8,128)(2,1)}, u32[]{:S(2)}) copy-start(bf16[256,128]{1,0:T(8,128)(2,1)} %constant.14.clone.table_ref.inv_two_ref) | copy-start | bytes 196612
  11.6 33.2 %all-to-all-start.2 = ((bf16[8,256,256]{2,1,0:T(8,128)(2,1)}), bf16[8,256,256]{2,1,0:T(8,128)(2,1)S(1)}, u32[]{:S(2)}, u32[]{:S(2)}) async-start(bf16[8,256,256]{2,1,0:T(8,128)(2,1)} %forward_zy.3), calls=%async_computation.2 | async-start | bytes 2097152 | tf_op jit(solution)/shard_map/all_to_all | solution.py:312
  19.0 88.6 %copy-start.9 = (bf16[4]{0:T(256)(128)(2,1)S(1)}, bf16[4]{0:T(256)(128)(2,1)}, u32[]{:S(2)}) copy-start(bf16[4]{0:T(256)(128)(2,1)} %param.9) | copy-start | bytes 28
  19.0 88.7 %copy-start.3 = (bf16[4,256,256]{2,1,0:T(8,128)(2,1)S(1)}, bf16[4,256,256]{2,1,0:T(8,128)(2,1)}, u32[]{:S(2)}) copy-start(bf16[4,256,256]{2,1,0:T(8,128)(2,1)} %constant.15.clone.inv_z_ref) | copy-start | bytes 1572868
  26.9 2.0 %copy-start = (bf16[2,4,4,4,128,128]{5,4,3,2,1,0:T(8,128)(2,1)}, bf16[2,4,4,4,128,128]{5,4,3,2,1,0:T(8,128)(2,1)S(1)}, u32[]{:S(2)}) copy-start(bf16[2,4,4,4,128,128]{5,4,3,2,1,0:T(8,128)(2,1)S(1)} %place_weights.1.w_ref) | copy-start | bytes 12582916
  44.8 29.5 %all-to-all-start = ((bf16[8,256,256]{2,1,0:T(8,128)(2,1)}), bf16[8,256,256]{2,1,0:T(8,128)(2,1)S(1)}, u32[]{:S(2)}, u32[]{:S(2)}) async-start(bf16[8,256,256]{2,1,0:T(8,128)(2,1)} %forward_zy.2), calls=%async_computation | async-start | bytes 2097152 | tf_op jit(solution)/shard_map/all_to_all | solution.py:312
  49.0 1.9 %collective-permute-start.6 = (bf16[128,256]{1,0:T(8,128)(2,1)S(1)}, bf16[128,256]{1,0:T(8,128)(2,1)S(1)}, u32[]{:S(2)}, u32[]{:S(2)}) collective-permute-start(bf16[128,256]{1,0:T(8,128)(2,1)S(1)} %get-tuple-element.34), channel_id=1, source_target_pairs={{0,1},{1,0},{2,3},{3,2},{4,5},{5,4},{6,7},{7,6},{8,9},{9,8},{10,11... | collective-permute-start | bytes 196616 | tf_op jit(solution)/shard_map/ppermute | solution.py:318
  49.1 4.5 %collective-permute-start.7 = (bf16[128,256]{1,0:T(8,128)(2,1)S(1)}, bf16[128,256]{1,0:T(8,128)(2,1)S(1)}, u32[]{:S(2)}, u32[]{:S(2)}) collective-permute-start(bf16[128,256]{1,0:T(8,128)(2,1)S(1)} %get-tuple-element.35), channel_id=1, source_target_pairs={{0,2},{1,3},{2,0},{3,1},{4,6},{5,7},{6,4},{7,5},{8,10},{9,11},{10,... | collective-permute-start | bytes 196616 | tf_op jit(solution)/shard_map/ppermute | solution.py:318
  50.6 4.0 %collective-permute-start.8 = (bf16[128,256]{1,0:T(8,128)(2,1)S(1)}, bf16[128,256]{1,0:T(8,128)(2,1)S(1)}, u32[]{:S(2)}, u32[]{:S(2)}) collective-permute-start(bf16[128,256]{1,0:T(8,128)(2,1)S(1)} %get-tuple-element.36), channel_id=1, source_target_pairs={{0,3},{1,2},{2,1},{3,0},{4,7},{5,6},{6,5},{7,4},{8,11},{9,10},{10,... | collective-permute-start | bytes 196616 | tf_op jit(solution)/shard_map/ppermute | solution.py:318
  54.7 2.2 %copy-start.1 = (bf16[2,4,4,4,128,128]{5,4,3,2,1,0:T(8,128)(2,1)S(1)}, bf16[2,4,4,4,128,128]{5,4,3,2,1,0:T(8,128)(2,1)}, u32[]{:S(2)}) copy-start(bf16[2,4,4,4,128,128]{5,4,3,2,1,0:T(8,128)(2,1)} %copy-done) | copy-start | bytes 12582916
  59.0 1.9 %collective-permute-start.9 = (bf16[128,256]{1,0:T(8,128)(2,1)S(1)}, bf16[128,256]{1,0:T(8,128)(2,1)S(1)}, u32[]{:S(2)}, u32[]{:S(2)}) collective-permute-start(bf16[128,256]{1,0:T(8,128)(2,1)S(1)} %get-tuple-element.38), channel_id=1, source_target_pairs={{0,1},{1,0},{2,3},{3,2},{4,5},{5,4},{6,7},{7,6},{8,9},{9,8},{10,11... | collective-permute-start | bytes 196616 | tf_op jit(solution)/shard_map/ppermute | solution.py:318
  59.4 4.3 %collective-permute-start.10 = (bf16[128,256]{1,0:T(8,128)(2,1)S(1)}, bf16[128,256]{1,0:T(8,128)(2,1)S(1)}, u32[]{:S(2)}, u32[]{:S(2)}) collective-permute-start(bf16[128,256]{1,0:T(8,128)(2,1)S(1)} %get-tuple-element.39), channel_id=1, source_target_pairs={{0,2},{1,3},{2,0},{3,1},{4,6},{5,7},{6,4},{7,5},{8,10},{9,11},{10,... | collective-permute-start | bytes 196616 | tf_op jit(solution)/shard_map/ppermute | solution.py:318
  60.9 4.4 %collective-permute-start.11 = (bf16[128,256]{1,0:T(8,128)(2,1)S(1)}, bf16[128,256]{1,0:T(8,128)(2,1)S(1)}, u32[]{:S(2)}, u32[]{:S(2)}) collective-permute-start(bf16[128,256]{1,0:T(8,128)(2,1)S(1)} %get-tuple-element.40), channel_id=1, source_target_pairs={{0,3},{1,2},{2,1},{3,0},{4,7},{5,6},{6,5},{7,4},{8,11},{9,10},{10,... | collective-permute-start | bytes 196616 | tf_op jit(solution)/shard_map/ppermute | solution.py:318
  74.3 29.6 %all-to-all-start.3 = ((bf16[8,256,256]{2,1,0:T(8,128)(2,1)}), bf16[8,256,256]{2,1,0:T(8,128)(2,1)S(1)}, u32[]{:S(2)}, u32[]{:S(2)}) async-start(bf16[8,256,256]{2,1,0:T(8,128)(2,1)} %inverse_x.3), calls=%async_computation.3 | async-start | bytes 2097152 | tf_op jit(solution)/shard_map/all_to_all | solution.py:312
  78.6 1.9 %collective-permute-start = (bf16[128,256]{1,0:T(8,128)(2,1)S(1)}, bf16[128,256]{1,0:T(8,128)(2,1)S(1)}, u32[]{:S(2)}, u32[]{:S(2)}) collective-permute-start(bf16[128,256]{1,0:T(8,128)(2,1)S(1)} %get-tuple-element.26), channel_id=1, source_target_pairs={{0,1},{1,0},{2,3},{3,2},{4,5},{5,4},{6,7},{7,6},{8,9},{9,8},{10,11... | collective-permute-start | bytes 196616 | tf_op jit(solution)/shard_map/ppermute | solution.py:318
  78.6 4.5 %collective-permute-start.1 = (bf16[128,256]{1,0:T(8,128)(2,1)S(1)}, bf16[128,256]{1,0:T(8,128)(2,1)S(1)}, u32[]{:S(2)}, u32[]{:S(2)}) collective-permute-start(bf16[128,256]{1,0:T(8,128)(2,1)S(1)} %get-tuple-element.27), channel_id=1, source_target_pairs={{0,2},{1,3},{2,0},{3,1},{4,6},{5,7},{6,4},{7,5},{8,10},{9,11},{10,... | collective-permute-start | bytes 196616 | tf_op jit(solution)/shard_map/ppermute | solution.py:318
  80.2 4.0 %collective-permute-start.2 = (bf16[128,256]{1,0:T(8,128)(2,1)S(1)}, bf16[128,256]{1,0:T(8,128)(2,1)S(1)}, u32[]{:S(2)}, u32[]{:S(2)}) collective-permute-start(bf16[128,256]{1,0:T(8,128)(2,1)S(1)} %get-tuple-element.28), channel_id=1, source_target_pairs={{0,3},{1,2},{2,1},{3,0},{4,7},{5,6},{6,5},{7,4},{8,11},{9,10},{10,... | collective-permute-start | bytes 196616 | tf_op jit(solution)/shard_map/ppermute | solution.py:318
  84.3 2.2 %copy-start.2 = (bf16[2,4,4,4,128,128]{5,4,3,2,1,0:T(8,128)(2,1)S(1)}, bf16[2,4,4,4,128,128]{5,4,3,2,1,0:T(8,128)(2,1)}, u32[]{:S(2)}) copy-start(bf16[2,4,4,4,128,128]{5,4,3,2,1,0:T(8,128)(2,1)} %copy-done) | copy-start | bytes 12582916
  88.6 1.9 %collective-permute-start.3 = (bf16[128,256]{1,0:T(8,128)(2,1)S(1)}, bf16[128,256]{1,0:T(8,128)(2,1)S(1)}, u32[]{:S(2)}, u32[]{:S(2)}) collective-permute-start(bf16[128,256]{1,0:T(8,128)(2,1)S(1)} %get-tuple-element.30), channel_id=1, source_target_pairs={{0,1},{1,0},{2,3},{3,2},{4,5},{5,4},{6,7},{7,6},{8,9},{9,8},{10,11... | collective-permute-start | bytes 196616 | tf_op jit(solution)/shard_map/ppermute | solution.py:318
  89.0 4.3 %collective-permute-start.4 = (bf16[128,256]{1,0:T(8,128)(2,1)S(1)}, bf16[128,256]{1,0:T(8,128)(2,1)S(1)}, u32[]{:S(2)}, u32[]{:S(2)}) collective-permute-start(bf16[128,256]{1,0:T(8,128)(2,1)S(1)} %get-tuple-element.31), channel_id=1, source_target_pairs={{0,2},{1,3},{2,0},{3,1},{4,6},{5,7},{6,4},{7,5},{8,10},{9,11},{10,... | collective-permute-start | bytes 196616 | tf_op jit(solution)/shard_map/ppermute | solution.py:318
  90.5 4.4 %collective-permute-start.5 = (bf16[128,256]{1,0:T(8,128)(2,1)S(1)}, bf16[128,256]{1,0:T(8,128)(2,1)S(1)}, u32[]{:S(2)}, u32[]{:S(2)}) collective-permute-start(bf16[128,256]{1,0:T(8,128)(2,1)S(1)} %get-tuple-element.32), channel_id=1, source_target_pairs={{0,3},{1,2},{2,1},{3,0},{4,7},{5,6},{6,5},{7,4},{8,11},{9,10},{10,... | collective-permute-start | bytes 196616 | tf_op jit(solution)/shard_map/ppermute | solution.py:318
  103.9 29.6 %all-to-all-start.1 = ((bf16[8,256,256]{2,1,0:T(8,128)(2,1)}), bf16[8,256,256]{2,1,0:T(8,128)(2,1)S(1)}, u32[]{:S(2)}, u32[]{:S(2)}) async-start(bf16[8,256,256]{2,1,0:T(8,128)(2,1)} %inverse_x.2), calls=%async_computation.1 | async-start | bytes 2097152 | tf_op jit(solution)/shard_map/all_to_all | solution.py:312

commit v4 on v3

--- a/solution.py
+++ b/solution.py
@@ -323,6 +323,7 @@
     samples, chans = state.shape[:2]
     fwd_z, fwd_two, inv_two, inv_z = make_tables(chans)
     shift = shift.astype(F32)
+    fwd_z, fwd_two = (pltpu.with_memory_space_constraint(t, pltpu.HBM) for t in (fwd_z, fwd_two))
     me = lax.axis_index("chan").reshape(1)
     placed = place_weights(jnp.transpose(weights, (0, 1, 2, 4, 5, 3)), me, chans)
     coef_y, back_x = [], []

time: 146 us -> 144 us (0.986)
  waiting for transfers between devices: 50.9 us -> 48.9 us
  local copies, waits for them, and re-layouts: 8.29 us -> 6.4 us
  Pallas kernels: 60.1 us -> 61.9 us
    all_to_all x4, waiting for transfers between devices: 34.8 us -> 32.7 us  [exchange(): return lax.all_to_all(blocks, axis, split_axis=0, concat_axis=0, tiled=True)]
    unnamed x20 -> x12, local copies, waits for them, and re-layouts: 8.29 us -> 6.4 us
    pallas_call x2, Pallas kernels: 1.23 us -> 2.9 us  [forward_x(): call(kernel, (4 * own * two * NG * lanes, 4 * slabs * rows * lanes), in_s...]
  transfers between devices with their start and end apart: 16 -> 16, of which waited for: 12 -> 12; matrix products, arithmetic and copies ran while one was open for 0% -> 0% of each run, Pallas kernels for 26% -> 28%
where the time goes in v4:
time: 144 us
  Pallas kernels  61.9 us (43%)
  waiting for transfers between devices  48.9 us (34%)
  starting transfers between devices  26.2 us (18%)
  local copies, waits for them, and re-layouts  6.4 us (4%)
    all_to_all x4, waiting for transfers between devices, exchange(): return lax.all_to_all(blocks, axis, split_axis=0, concat_axis=0, tiled=True)  32.7 us
    pallas_call x2, Pallas kernels, inverse_yz(): call(kernel, (2 * planes * NG * (2 * two * lanes + chans * lanes * NG), 2...  23.9 us
    pallas_call x2, Pallas kernels, forward_zy(): call(kernel, (2 * planes * NG * lanes * (chans * NG + 2 * two), 2 * chans...  19.5 us
    all_to_all x4, starting transfers between devices, exchange(): return lax.all_to_all(blocks, axis, split_axis=0, concat_axis=0, tiled=True)  18.4 us
    ppermute x12, waiting for transfers between devices, swap(): lax.ppermute(blocks[r], axis, [(i, i ^ r) for i in range(count)])  16.2 us
    pallas_call x1, Pallas kernels, place_weights(): call(kernel, (2 * weights.size, 10 * weights.size), grid_spec=pltpu.Prefe...  7.87 us
    ppermute x12, starting transfers between devices, swap(): lax.ppermute(blocks[r], axis, [(i, i ^ r) for i in range(count)])  7.86 us
    unnamed x12, local copies, waits for them, and re-layouts  6.4 us
  transfers between devices with their start and end apart: 16, of which 12 were waited for; matrix products, arithmetic and copies ran while one was open for 0% of the time, Pallas kernels for 28%

profile of v4, /device:TPU:0, one launch (start us, length us, event | category | flops | bytes accessed | tf_op | source)
XLA Modules:
  0.0 143.6 jit_solution(2745172623936856156)
XLA Ops:
  0.0 9.8 %forward_zy.3 = bf16[8,256,256]{2,1,0:T(8,128)(2,1)} custom-call(bf16[2,4,32,256,256]{4,3,2,1,0:T(8,128)(2,1)} %state_ref.3, bf16[1024,256]{1,0:T(8,128)(2,1)} %constant.12.clone.fwd_z_ref, bf16[128,256]{1,0:T(8,128)(2,1)} %constant.13.clone.fwd_two_ref.table_ref), custom_call_target="tpu_custom_call" | custom-call | flops 4831838208 | bytes 16777216 | tf_op jit(solution)/shard_map/forward_zy/pallas_call | solution.py:97
  9.8 0.0 copy-start.4
  9.8 7.4 %all-to-all-start.2 = ((bf16[8,256,256]{2,1,0:T(8,128)(2,1)}), bf16[8,256,256]{2,1,0:T(8,128)(2,1)S(1)}, u32[]{:S(2)}, u32[]{:S(2)}) async-start(bf16[8,256,256]{2,1,0:T(8,128)(2,1)} %forward_zy.3), calls=%async_computation.2 | async-start | bytes 2097152 | tf_op jit(solution)/shard_map/all_to_all | solution.py:312
  17.2 0.0 copy-start.5
  17.2 0.0 copy-start.3
  17.2 7.9 %place_weights.1.w_ref = bf16[2,4,4,4,128,128]{5,4,3,2,1,0:T(8,128)(2,1)S(1)} custom-call(s32[1]{0:T(128)} %bitcast.me_ref, bf16[16,16,16,2,8,32]{5,4,3,2,1,0:T(8,128)(2,1)} %bitcast.2), custom_call_target="tpu_custom_call" | custom-call | flops 4194304 | bytes 20971520 | tf_op jit(solution)/shard_map/place_weights/pallas_call | solution.py:170
  25.1 0.0 copy-start
  25.1 2.0 %copy-done = bf16[2,4,4,4,128,128]{5,4,3,2,1,0:T(8,128)(2,1)} copy-done((bf16[2,4,4,4,128,128]{5,4,3,2,1,0:T(8,128)(2,1)}, bf16[2,4,4,4,128,128]{5,4,3,2,1,0:T(8,128)(2,1)S(1)}, u32[]{:S(2)}) %copy-start) | copy-done | bytes 4194328
  27.1 9.8 %forward_zy.2 = bf16[8,256,256]{2,1,0:T(8,128)(2,1)} custom-call(bf16[2,4,32,256,256]{4,3,2,1,0:T(8,128)(2,1)} %state_ref.3, bf16[1024,256]{1,0:T(8,128)(2,1)} %constant.12.clone.fwd_z_ref, bf16[128,256]{1,0:T(8,128)(2,1)} %constant.13.clone.fwd_two_ref.table_ref), custom_call_target="tpu_custom_call" | custom-call | flops 4831838208 | bytes 16777216 | tf_op jit(solution)/shard_map/forward_zy/pallas_call | solution.py:97
  36.9 6.1 %all-to-all-done.2.coef_ref = bf16[8,256,256]{2,1,0:T(8,128)(2,1)S(1)} async-done(((bf16[8,256,256]{2,1,0:T(8,128)(2,1)}), bf16[8,256,256]{2,1,0:T(8,128)(2,1)S(1)}, u32[]{:S(2)}, u32[]{:S(2)}) %all-to-all-start.2) | async-done | bytes 1048608 | tf_op jit(solution)/shard_map/all_to_all | solution.py:312
  42.9 3.6 %all-to-all-start = ((bf16[8,256,256]{2,1,0:T(8,128)(2,1)}), bf16[8,256,256]{2,1,0:T(8,128)(2,1)S(1)}, u32[]{:S(2)}, u32[]{:S(2)}) async-start(bf16[8,256,256]{2,1,0:T(8,128)(2,1)} %forward_zy.2), calls=%async_computation | async-start | bytes 2097152 | tf_op jit(solution)/shard_map/all_to_all | solution.py:312
  46.5 1.4 %forward_x.3 = (bf16[128,256]{1,0:T(8,128)(2,1)S(1)}, bf16[128,256]{1,0:T(8,128)(2,1)S(1)}, bf16[128,256]{1,0:T(8,128)(2,1)S(1)}, bf16[128,256]{1,0:T(8,128)(2,1)S(1)}) custom-call(s32[1]{0:T(128)} %bitcast.me_ref, bf16[8,256,256]{2,1,0:T(8,128)(2,1)S(1)} %all-to-all-done.2.coef_ref, bf16[128,256]{1,0:T(8,128)(2,1)} %constant.13.clone.fwd_two_ref.table_ref), custom_call_target="tpu_custom_call" | custom-call | flops 134217728 | bytes 2097152 | tf_op jit(solution)/shard_map/forward_x/pallas_call | solution.py:138
  48.0 0.1 collective-permute-start.6
  48.1 1.6 %collective-permute-start.7 = (bf16[128,256]{1,0:T(8,128)(2,1)S(1)}, bf16[128,256]{1,0:T(8,128)(2,1)S(1)}, u32[]{:S(2)}, u32[]{:S(2)}) collective-permute-start(bf16[128,256]{1,0:T(8,128)(2,1)S(1)} %get-tuple-element.35), channel_id=1, source_target_pairs={{0,2},{1,3},{2,0},{3,1},{4,6},{5,7},{6,4},{7,5},{8,10},{9,11},{10,... | collective-permute-start | bytes 196616 | tf_op jit(solution)/shard_map/ppermute | solution.py:318
  49.6 0.3 collective-permute-start.8
  49.9 0.0 collective-permute-done.6.refs_1_
  49.9 2.6 %collective-permute-done.7.refs_2_ = bf16[128,256]{1,0:T(8,128)(2,1)S(1)} collective-permute-done((bf16[128,256]{1,0:T(8,128)(2,1)S(1)}, bf16[128,256]{1,0:T(8,128)(2,1)S(1)}, u32[]{:S(2)}, u32[]{:S(2)}) %collective-permute-start.7) | collective-permute-done | bytes 65568 | tf_op jit(solution)/shard_map/ppermute | solution.py:318
  52.6 1.1 collective-permute-done.8.refs_3_
  53.7 0.0 copy-start.1
  53.7 2.2 %copy-done.1 = bf16[2,4,4,4,128,128]{5,4,3,2,1,0:T(8,128)(2,1)S(1)} copy-done((bf16[2,4,4,4,128,128]{5,4,3,2,1,0:T(8,128)(2,1)S(1)}, bf16[2,4,4,4,128,128]{5,4,3,2,1,0:T(8,128)(2,1)}, u32[]{:S(2)}) %copy-start.1) | copy-done | bytes 4194328
  55.9 2.2 %mix.3 = (bf16[128,256]{1,0:T(8,128)(2,1)S(1)}, bf16[128,256]{1,0:T(8,128)(2,1)S(1)}, bf16[128,256]{1,0:T(8,128)(2,1)S(1)}, bf16[128,256]{1,0:T(8,128)(2,1)S(1)}) custom-call(bf16[2,4,4,4,128,128]{5,4,3,2,1,0:T(8,128)(2,1)S(1)} %copy-done.1, bf16[128,256]{1,0:T(8,128)(2,1)S(1)} %get-tuple-element.33.refs_0_, ...), custom_call_target="tpu_custom_call" | custom-call | flops 8388608 | bytes 4194304 | tf_op jit(solution)/shard_map/mix/pallas_call | solution.py:218
  58.1 0.5 collective-permute-start.9
  58.6 1.5 %collective-permute-start.10 = (bf16[128,256]{1,0:T(8,128)(2,1)S(1)}, bf16[128,256]{1,0:T(8,128)(2,1)S(1)}, u32[]{:S(2)}, u32[]{:S(2)}) collective-permute-start(bf16[128,256]{1,0:T(8,128)(2,1)S(1)} %get-tuple-element.39), channel_id=1, source_target_pairs={{0,2},{1,3},{2,0},{3,1},{4,6},{5,7},{6,4},{7,5},{8,10},{9,11},{10,... | collective-permute-start | bytes 196616 | tf_op jit(solution)/shard_map/ppermute | solution.py:318
  60.0 0.0 collective-permute-start.11
  60.1 0.0 collective-permute-done.9.refs_1_
  60.1 2.8 %collective-permute-done.10.refs_2_ = bf16[128,256]{1,0:T(8,128)(2,1)S(1)} collective-permute-done((bf16[128,256]{1,0:T(8,128)(2,1)S(1)}, bf16[128,256]{1,0:T(8,128)(2,1)S(1)}, u32[]{:S(2)}, u32[]{:S(2)}) %collective-permute-start.10) | collective-permute-done | bytes 65568 | tf_op jit(solution)/shard_map/ppermute | solution.py:318
  62.8 1.6 %collective-permute-done.11.refs_3_ = bf16[128,256]{1,0:T(8,128)(2,1)S(1)} collective-permute-done((bf16[128,256]{1,0:T(8,128)(2,1)S(1)}, bf16[128,256]{1,0:T(8,128)(2,1)S(1)}, u32[]{:S(2)}, u32[]{:S(2)}) %collective-permute-start.11) | collective-permute-done | bytes 65568 | tf_op jit(solution)/shard_map/ppermute | solution.py:318
  64.4 0.0 copy-done.4
  64.4 1.7 %inverse_x.3 = bf16[8,256,256]{2,1,0:T(8,128)(2,1)} custom-call(s32[1]{0:T(128)} %bitcast.me_ref, bf16[256,128]{1,0:T(8,128)(2,1)S(1)} %copy-done.4, bf16[128,256]{1,0:T(8,128)(2,1)S(1)} %get-tuple-element.37.refs_0_, bf16[128,256]{1,0:T(8,128)(2,1)S(1)} %collective-permute-done.9.refs_1_, bf16[128,256]{1,0:T(8,128)(2,1)S(1)} %collective-permute-done.10.refs_2_, ...), custom_call_target="tpu_custom_call" | custom-call | flops 134217728 | bytes 2097152 | tf_op jit(solution)/shard_map/inverse_x/pallas_call | solution.py:255
  66.1 6.4 %all-to-all-done.coef_ref = bf16[8,256,256]{2,1,0:T(8,128)(2,1)S(1)} async-done(((bf16[8,256,256]{2,1,0:T(8,128)(2,1)}), bf16[8,256,256]{2,1,0:T(8,128)(2,1)S(1)}, u32[]{:S(2)}, u32[]{:S(2)}) %all-to-all-start) | async-done | bytes 1048608 | tf_op jit(solution)/shard_map/all_to_all | solution.py:312
  72.5 3.6 %all-to-all-start.3 = ((bf16[8,256,256]{2,1,0:T(8,128)(2,1)}), bf16[8,256,256]{2,1,0:T(8,128)(2,1)S(1)}, u32[]{:S(2)}, u32[]{:S(2)}) async-start(bf16[8,256,256]{2,1,0:T(8,128)(2,1)} %inverse_x.3), calls=%async_computation.3 | async-start | bytes 2097152 | tf_op jit(solution)/shard_map/all_to_all | solution.py:312
  76.1 1.4 %forward_x.2 = (bf16[128,256]{1,0:T(8,128)(2,1)S(1)}, bf16[128,256]{1,0:T(8,128)(2,1)S(1)}, bf16[128,256]{1,0:T(8,128)(2,1)S(1)}, bf16[128,256]{1,0:T(8,128)(2,1)S(1)}) custom-call(s32[1]{0:T(128)} %bitcast.me_ref, bf16[8,256,256]{2,1,0:T(8,128)(2,1)S(1)} %all-to-all-done.coef_ref, bf16[128,256]{1,0:T(8,128)(2,1)} %constant.13.clone.fwd_two_ref.table_ref), custom_call_target="tpu_custom_call" | custom-call | flops 134217728 | bytes 2097152 | tf_op jit(solution)/shard_map/forward_x/pallas_call | solution.py:138
  77.6 0.1 collective-permute-start
  77.6 1.6 %collective-permute-start.1 = (bf16[128,256]{1,0:T(8,128)(2,1)S(1)}, bf16[128,256]{1,0:T(8,128)(2,1)S(1)}, u32[]{:S(2)}, u32[]{:S(2)}) collective-permute-start(bf16[128,256]{1,0:T(8,128)(2,1)S(1)} %get-tuple-element.27), channel_id=1, source_target_pairs={{0,2},{1,3},{2,0},{3,1},{4,6},{5,7},{6,4},{7,5},{8,10},{9,11},{10,... | collective-permute-start | bytes 196616 | tf_op jit(solution)/shard_map/ppermute | solution.py:318
  79.2 0.3 collective-permute-start.2
  79.5 0.0 collective-permute-done.refs_1_
  79.5 2.6 %collective-permute-done.1.refs_2_ = bf16[128,256]{1,0:T(8,128)(2,1)S(1)} collective-permute-done((bf16[128,256]{1,0:T(8,128)(2,1)S(1)}, bf16[128,256]{1,0:T(8,128)(2,1)S(1)}, u32[]{:S(2)}, u32[]{:S(2)}) %collective-permute-start.1) | collective-permute-done | bytes 65568 | tf_op jit(solution)/shard_map/ppermute | solution.py:318
  82.2 1.1 collective-permute-done.2.refs_3_
  83.3 0.0 copy-start.2
  83.3 2.2 %copy-done.2 = bf16[2,4,4,4,128,128]{5,4,3,2,1,0:T(8,128)(2,1)S(1)} copy-done((bf16[2,4,4,4,128,128]{5,4,3,2,1,0:T(8,128)(2,1)S(1)}, bf16[2,4,4,4,128,128]{5,4,3,2,1,0:T(8,128)(2,1)}, u32[]{:S(2)}) %copy-start.2) | copy-done | bytes 4194328
  85.4 2.2 %mix.2 = (bf16[128,256]{1,0:T(8,128)(2,1)S(1)}, bf16[128,256]{1,0:T(8,128)(2,1)S(1)}, bf16[128,256]{1,0:T(8,128)(2,1)S(1)}, bf16[128,256]{1,0:T(8,128)(2,1)S(1)}) custom-call(bf16[2,4,4,4,128,128]{5,4,3,2,1,0:T(8,128)(2,1)S(1)} %copy-done.2, bf16[128,256]{1,0:T(8,128)(2,1)S(1)} %get-tuple-element.25.refs_0_, ...), custom_call_target="tpu_custom_call" | custom-call | flops 8388608 | bytes 4194304 | tf_op jit(solution)/shard_map/mix/pallas_call | solution.py:218
  87.6 0.5 collective-permute-start.3
  88.2 1.5 %collective-permute-start.4 = (bf16[128,256]{1,0:T(8,128)(2,1)S(1)}, bf16[128,256]{1,0:T(8,128)(2,1)S(1)}, u32[]{:S(2)}, u32[]{:S(2)}) collective-permute-start(bf16[128,256]{1,0:T(8,128)(2,1)S(1)} %get-tuple-element.31), channel_id=1, source_target_pairs={{0,2},{1,3},{2,0},{3,1},{4,6},{5,7},{6,4},{7,5},{8,10},{9,11},{10,... | collective-permute-start | bytes 196616 | tf_op jit(solution)/shard_map/ppermute | solution.py:318
  89.6 0.0 collective-permute-start.5
  89.6 0.0 collective-permute-done.3.refs_1_
  89.6 2.8 %collective-permute-done.4.refs_2_ = bf16[128,256]{1,0:T(8,128)(2,1)S(1)} collective-permute-done((bf16[128,256]{1,0:T(8,128)(2,1)S(1)}, bf16[128,256]{1,0:T(8,128)(2,1)S(1)}, u32[]{:S(2)}, u32[]{:S(2)}) %collective-permute-start.4) | collective-permute-done | bytes 65568 | tf_op jit(solution)/shard_map/ppermute | solution.py:318
  92.4 1.6 %collective-permute-done.5.refs_3_ = bf16[128,256]{1,0:T(8,128)(2,1)S(1)} collective-permute-done((bf16[128,256]{1,0:T(8,128)(2,1)S(1)}, bf16[128,256]{1,0:T(8,128)(2,1)S(1)}, u32[]{:S(2)}, u32[]{:S(2)}) %collective-permute-start.5) | collective-permute-done | bytes 65568 | tf_op jit(solution)/shard_map/ppermute | solution.py:318
  94.0 1.6 %inverse_x.2 = bf16[8,256,256]{2,1,0:T(8,128)(2,1)} custom-call(s32[1]{0:T(128)} %bitcast.me_ref, bf16[256,128]{1,0:T(8,128)(2,1)S(1)} %copy-done.4, bf16[128,256]{1,0:T(8,128)(2,1)S(1)} %get-tuple-element.29.refs_0_, bf16[128,256]{1,0:T(8,128)(2,1)S(1)} %collective-permute-done.3.refs_1_, bf16[128,256]{1,0:T(8,128)(2,1)S(1)} %collective-permute-done.4.refs_2_, ...), custom_call_target="tpu_custom_call" | custom-call | flops 134217728 | bytes 2097152 | tf_op jit(solution)/shard_map/inverse_x/pallas_call | solution.py:255
  95.6 6.4 %all-to-all-done.3.back_ref = bf16[8,256,256]{2,1,0:T(8,128)(2,1)S(1)} async-done(((bf16[8,256,256]{2,1,0:T(8,128)(2,1)}), bf16[8,256,256]{2,1,0:T(8,128)(2,1)S(1)}, u32[]{:S(2)}, u32[]{:S(2)}) %all-to-all-start.3) | async-done | bytes 1048608 | tf_op jit(solution)/shard_map/all_to_all | solution.py:312
  102.1 3.7 %all-to-all-start.1 = ((bf16[8,256,256]{2,1,0:T(8,128)(2,1)}), bf16[8,256,256]{2,1,0:T(8,128)(2,1)S(1)}, u32[]{:S(2)}, u32[]{:S(2)}) async-start(bf16[8,256,256]{2,1,0:T(8,128)(2,1)} %inverse_x.2), calls=%async_computation.1 | async-start | bytes 2097152 | tf_op jit(solution)/shard_map/all_to_all | solution.py:312
  105.8 0.0 copy-done.5
  105.8 0.0 copy-done.3
  105.8 12.0 %inverse_yz.2.refs_0_ = bf16[2,4,32,256,256]{4,3,2,1,0:T(8,128)(2,1)} custom-call(bf16[8,256,256]{2,1,0:T(8,128)(2,1)S(1)} %all-to-all-done.3.back_ref, f32[4]{0:T(128)S(1)} %convert_element_type.3.shift_ref, bf16[256,128]{1,0:T(8,128)(2,1)S(1)} %copy-done.4, bf16[4,256,256]{2,1,0:T(8,128)(2,1)S(1)} %copy-done.3), custom_call_target="tpu_custom_call" | custom-call | flops 4831838208 | bytes 16777216 | tf_op jit(solution)/shard_map/inverse_yz/pallas_call | solution.py:292
  117.8 13.8 %all-to-all-done.1.back_ref = bf16[8,256,256]{2,1,0:T(8,128)(2,1)S(1)} async-done(((bf16[8,256,256]{2,1,0:T(8,128)(2,1)}), bf16[8,256,256]{2,1,0:T(8,128)(2,1)S(1)}, u32[]{:S(2)}, u32[]{:S(2)}) %all-to-all-start.1) | async-done | bytes 1048608 | tf_op jit(solution)/shard_map/all_to_all | solution.py:312
  131.7 12.0 %inverse_yz.3 = bf16[2,4,32,256,256]{4,3,2,1,0:T(8,128)(2,1)} custom-call(bf16[8,256,256]{2,1,0:T(8,128)(2,1)S(1)} %all-to-all-done.1.back_ref, f32[4]{0:T(128)S(1)} %convert_element_type.3.shift_ref, bf16[256,128]{1,0:T(8,128)(2,1)S(1)} %copy-done.4, bf16[4,256,256]{2,1,0:T(8,128)(2,1)S(1)} %copy-done.3, ...), custom_call_target="tpu_custom_call", output_to_operand_aliasing={{}: (4, {})} | custom-call | flops 4831838208 | bytes 16777216 | tf_op jit(solution)/shard_map/inverse_yz/pallas_call | solution.py:292
  (1 shorter events, 0.0 us)
Async XLA Ops:
  9.8 54.7 %copy-start.4 = (bf16[256,128]{1,0:T(8,128)(2,1)S(1)}, bf16[256,128]{1,0:T(8,128)(2,1)}, u32[]{:S(2)}) copy-start(bf16[256,128]{1,0:T(8,128)(2,1)} %constant.14.clone.table_ref.inv_two_ref) | copy-start | bytes 196612
  9.8 33.2 %all-to-all-start.2 = ((bf16[8,256,256]{2,1,0:T(8,128)(2,1)}), bf16[8,256,256]{2,1,0:T(8,128)(2,1)S(1)}, u32[]{:S(2)}, u32[]{:S(2)}) async-start(bf16[8,256,256]{2,1,0:T(8,128)(2,1)} %forward_zy.3), calls=%async_computation.2 | async-start | bytes 2097152 | tf_op jit(solution)/shard_map/all_to_all | solution.py:312
  17.2 88.6 %copy-start.5 = (bf16[4]{0:T(256)(128)(2,1)S(1)}, bf16[4]{0:T(256)(128)(2,1)}, u32[]{:S(2)}) copy-start(bf16[4]{0:T(256)(128)(2,1)} %param.9) | copy-start | bytes 28
  17.2 88.7 %copy-start.3 = (bf16[4,256,256]{2,1,0:T(8,128)(2,1)S(1)}, bf16[4,256,256]{2,1,0:T(8,128)(2,1)}, u32[]{:S(2)}) copy-start(bf16[4,256,256]{2,1,0:T(8,128)(2,1)} %constant.15.clone.inv_z_ref) | copy-start | bytes 1572868
  25.1 2.0 %copy-start = (bf16[2,4,4,4,128,128]{5,4,3,2,1,0:T(8,128)(2,1)}, bf16[2,4,4,4,128,128]{5,4,3,2,1,0:T(8,128)(2,1)S(1)}, u32[]{:S(2)}) copy-start(bf16[2,4,4,4,128,128]{5,4,3,2,1,0:T(8,128)(2,1)S(1)} %place_weights.1.w_ref) | copy-start | bytes 12582916
  42.9 29.5 %all-to-all-start = ((bf16[8,256,256]{2,1,0:T(8,128)(2,1)}), bf16[8,256,256]{2,1,0:T(8,128)(2,1)S(1)}, u32[]{:S(2)}, u32[]{:S(2)}) async-start(bf16[8,256,256]{2,1,0:T(8,128)(2,1)} %forward_zy.2), calls=%async_computation | async-start | bytes 2097152 | tf_op jit(solution)/shard_map/all_to_all | solution.py:312
  48.0 1.9 %collective-permute-start.6 = (bf16[128,256]{1,0:T(8,128)(2,1)S(1)}, bf16[128,256]{1,0:T(8,128)(2,1)S(1)}, u32[]{:S(2)}, u32[]{:S(2)}) collective-permute-start(bf16[128,256]{1,0:T(8,128)(2,1)S(1)} %get-tuple-element.34), channel_id=1, source_target_pairs={{0,1},{1,0},{2,3},{3,2},{4,5},{5,4},{6,7},{7,6},{8,9},{9,8},{10,11... | collective-permute-start | bytes 196616 | tf_op jit(solution)/shard_map/ppermute | solution.py:318
  48.1 4.5 %collective-permute-start.7 = (bf16[128,256]{1,0:T(8,128)(2,1)S(1)}, bf16[128,256]{1,0:T(8,128)(2,1)S(1)}, u32[]{:S(2)}, u32[]{:S(2)}) collective-permute-start(bf16[128,256]{1,0:T(8,128)(2,1)S(1)} %get-tuple-element.35), channel_id=1, source_target_pairs={{0,2},{1,3},{2,0},{3,1},{4,6},{5,7},{6,4},{7,5},{8,10},{9,11},{10,... | collective-permute-start | bytes 196616 | tf_op jit(solution)/shard_map/ppermute | solution.py:318
  49.6 4.0 %collective-permute-start.8 = (bf16[128,256]{1,0:T(8,128)(2,1)S(1)}, bf16[128,256]{1,0:T(8,128)(2,1)S(1)}, u32[]{:S(2)}, u32[]{:S(2)}) collective-permute-start(bf16[128,256]{1,0:T(8,128)(2,1)S(1)} %get-tuple-element.36), channel_id=1, source_target_pairs={{0,3},{1,2},{2,1},{3,0},{4,7},{5,6},{6,5},{7,4},{8,11},{9,10},{10,... | collective-permute-start | bytes 196616 | tf_op jit(solution)/shard_map/ppermute | solution.py:318
  53.7 2.2 %copy-start.1 = (bf16[2,4,4,4,128,128]{5,4,3,2,1,0:T(8,128)(2,1)S(1)}, bf16[2,4,4,4,128,128]{5,4,3,2,1,0:T(8,128)(2,1)}, u32[]{:S(2)}) copy-start(bf16[2,4,4,4,128,128]{5,4,3,2,1,0:T(8,128)(2,1)} %copy-done) | copy-start | bytes 12582916
  58.1 2.0 %collective-permute-start.9 = (bf16[128,256]{1,0:T(8,128)(2,1)S(1)}, bf16[128,256]{1,0:T(8,128)(2,1)S(1)}, u32[]{:S(2)}, u32[]{:S(2)}) collective-permute-start(bf16[128,256]{1,0:T(8,128)(2,1)S(1)} %get-tuple-element.38), channel_id=1, source_target_pairs={{0,1},{1,0},{2,3},{3,2},{4,5},{5,4},{6,7},{7,6},{8,9},{9,8},{10,11... | collective-permute-start | bytes 196616 | tf_op jit(solution)/shard_map/ppermute | solution.py:318
  58.6 4.3 %collective-permute-start.10 = (bf16[128,256]{1,0:T(8,128)(2,1)S(1)}, bf16[128,256]{1,0:T(8,128)(2,1)S(1)}, u32[]{:S(2)}, u32[]{:S(2)}) collective-permute-start(bf16[128,256]{1,0:T(8,128)(2,1)S(1)} %get-tuple-element.39), channel_id=1, source_target_pairs={{0,2},{1,3},{2,0},{3,1},{4,6},{5,7},{6,4},{7,5},{8,10},{9,11},{10,... | collective-permute-start | bytes 196616 | tf_op jit(solution)/shard_map/ppermute | solution.py:318
  60.0 4.4 %collective-permute-start.11 = (bf16[128,256]{1,0:T(8,128)(2,1)S(1)}, bf16[128,256]{1,0:T(8,128)(2,1)S(1)}, u32[]{:S(2)}, u32[]{:S(2)}) collective-permute-start(bf16[128,256]{1,0:T(8,128)(2,1)S(1)} %get-tuple-element.40), channel_id=1, source_target_pairs={{0,3},{1,2},{2,1},{3,0},{4,7},{5,6},{6,5},{7,4},{8,11},{9,10},{10,... | collective-permute-start | bytes 196616 | tf_op jit(solution)/shard_map/ppermute | solution.py:318
  72.5 29.6 %all-to-all-start.3 = ((bf16[8,256,256]{2,1,0:T(8,128)(2,1)}), bf16[8,256,256]{2,1,0:T(8,128)(2,1)S(1)}, u32[]{:S(2)}, u32[]{:S(2)}) async-start(bf16[8,256,256]{2,1,0:T(8,128)(2,1)} %inverse_x.3), calls=%async_computation.3 | async-start | bytes 2097152 | tf_op jit(solution)/shard_map/all_to_all | solution.py:312
  77.6 1.9 %collective-permute-start = (bf16[128,256]{1,0:T(8,128)(2,1)S(1)}, bf16[128,256]{1,0:T(8,128)(2,1)S(1)}, u32[]{:S(2)}, u32[]{:S(2)}) collective-permute-start(bf16[128,256]{1,0:T(8,128)(2,1)S(1)} %get-tuple-element.26), channel_id=1, source_target_pairs={{0,1},{1,0},{2,3},{3,2},{4,5},{5,4},{6,7},{7,6},{8,9},{9,8},{10,11... | collective-permute-start | bytes 196616 | tf_op jit(solution)/shard_map/ppermute | solution.py:318
  77.6 4.5 %collective-permute-start.1 = (bf16[128,256]{1,0:T(8,128)(2,1)S(1)}, bf16[128,256]{1,0:T(8,128)(2,1)S(1)}, u32[]{:S(2)}, u32[]{:S(2)}) collective-permute-start(bf16[128,256]{1,0:T(8,128)(2,1)S(1)} %get-tuple-element.27), channel_id=1, source_target_pairs={{0,2},{1,3},{2,0},{3,1},{4,6},{5,7},{6,4},{7,5},{8,10},{9,11},{10,... | collective-permute-start | bytes 196616 | tf_op jit(solution)/shard_map/ppermute | solution.py:318
  79.2 4.0 %collective-permute-start.2 = (bf16[128,256]{1,0:T(8,128)(2,1)S(1)}, bf16[128,256]{1,0:T(8,128)(2,1)S(1)}, u32[]{:S(2)}, u32[]{:S(2)}) collective-permute-start(bf16[128,256]{1,0:T(8,128)(2,1)S(1)} %get-tuple-element.28), channel_id=1, source_target_pairs={{0,3},{1,2},{2,1},{3,0},{4,7},{5,6},{6,5},{7,4},{8,11},{9,10},{10,... | collective-permute-start | bytes 196616 | tf_op jit(solution)/shard_map/ppermute | solution.py:318
  83.3 2.2 %copy-start.2 = (bf16[2,4,4,4,128,128]{5,4,3,2,1,0:T(8,128)(2,1)S(1)}, bf16[2,4,4,4,128,128]{5,4,3,2,1,0:T(8,128)(2,1)}, u32[]{:S(2)}) copy-start(bf16[2,4,4,4,128,128]{5,4,3,2,1,0:T(8,128)(2,1)} %copy-done) | copy-start | bytes 12582916
  87.6 2.0 %collective-permute-start.3 = (bf16[128,256]{1,0:T(8,128)(2,1)S(1)}, bf16[128,256]{1,0:T(8,128)(2,1)S(1)}, u32[]{:S(2)}, u32[]{:S(2)}) collective-permute-start(bf16[128,256]{1,0:T(8,128)(2,1)S(1)} %get-tuple-element.30), channel_id=1, source_target_pairs={{0,1},{1,0},{2,3},{3,2},{4,5},{5,4},{6,7},{7,6},{8,9},{9,8},{10,11... | collective-permute-start | bytes 196616 | tf_op jit(solution)/shard_map/ppermute | solution.py:318
  88.2 4.3 %collective-permute-start.4 = (bf16[128,256]{1,0:T(8,128)(2,1)S(1)}, bf16[128,256]{1,0:T(8,128)(2,1)S(1)}, u32[]{:S(2)}, u32[]{:S(2)}) collective-permute-start(bf16[128,256]{1,0:T(8,128)(2,1)S(1)} %get-tuple-element.31), channel_id=1, source_target_pairs={{0,2},{1,3},{2,0},{3,1},{4,6},{5,7},{6,4},{7,5},{8,10},{9,11},{10,... | collective-permute-start | bytes 196616 | tf_op jit(solution)/shard_map/ppermute | solution.py:318
  89.6 4.4 %collective-permute-start.5 = (bf16[128,256]{1,0:T(8,128)(2,1)S(1)}, bf16[128,256]{1,0:T(8,128)(2,1)S(1)}, u32[]{:S(2)}, u32[]{:S(2)}) collective-permute-start(bf16[128,256]{1,0:T(8,128)(2,1)S(1)} %get-tuple-element.32), channel_id=1, source_target_pairs={{0,3},{1,2},{2,1},{3,0},{4,7},{5,6},{6,5},{7,4},{8,11},{9,10},{10,... | collective-permute-start | bytes 196616 | tf_op jit(solution)/shard_map/ppermute | solution.py:318
  102.1 29.6 %all-to-all-start.1 = ((bf16[8,256,256]{2,1,0:T(8,128)(2,1)}), bf16[8,256,256]{2,1,0:T(8,128)(2,1)S(1)}, u32[]{:S(2)}, u32[]{:S(2)}) async-start(bf16[8,256,256]{2,1,0:T(8,128)(2,1)} %inverse_x.2), calls=%async_computation.1 | async-start | bytes 2097152 | tf_op jit(solution)/shard_map/all_to_all | solution.py:312
